TPU v7x, 768 devices: a whole 4x8x12 slice. The times are simulated.
768 devices in a mesh: panel: 6 (over z_lo), tile: 16 (over x, z_hi, core), lev: 8 (over y).
Axes of the slice: x: 4, y: 8, z: 12 (z_hi: 2, z_lo: 6; z = z_hi * 6 + z_lo), core: 2. Of those that a mesh axis runs over, the one named last changes fastest.
Arguments:
- parent: float32 [6, 8, 4, 512, 512], P('panel', 'lev', None, 'tile'), may hold values from -6 to 6
- courant: float32 [6, 8, 3, 512, 512], P('panel', 'lev', None, 'tile'), may hold values from 0.02 to 0.2
- edge_links: int32 [6, 4, 3], replicated, may hold values from 0 to 5, as said below
- nest_tracer: float32 [6, 64, 8, 4, 4096], P('panel', 'tile', 'lev'), may hold values from -6 to 6
- nest_weight: float32 [6, 64, 4096], P('panel', 'tile'), may hold values from 0.05 to 0.25
- nest_map: int32 [6, 64, 4096], P('panel', 'tile'), may hold values from 0 to 262143, as said below
- block_live: int32 [6, 64], P('panel', 'tile'), may hold values 0 or 1
Outputs:
- updated: float32 [6, 8, 4, 512, 512], P('panel', 'lev', None, 'tile')
Inputs may be any that keep to these rules, and one draw needn't show every extreme that they name: `edge_links`: each side is paired with one other side, and the pairing is symmetric: if side s of panel p names (q, r, f), side r of panel q names (p, s, f). `nest_map`: nest cell (i, j) of a 64 x 64 block, at position i * 64 + j, maps to parent cell (a + i // 3) * 512 + b + j // 3 of the same panel for a corner (a, b) of that block; blocks may intersect.
All inputs are finite; a program needn't handle non-finite values. No bound on the sum of `block_live` on one device may be relied on, other than what follows from the above.
Results may differ from a plain program's by a relative error of at most 0.00002.
Values sent between devices are 32-bit elements; how exact they have to be, the bound alone decides.
No kernel may reach another device: no remote copies, remote signals or barrier semaphores. Data moves between devices by JAX's collectives and lax.ppermute only.
A program may use at most 64 MiB of HBM per device.

v0:
```python
import jax
import jax.numpy as jnp
from jax import lax
from jax.sharding import PartitionSpec as P

BEDGE = 64
WIN = 22


def extended(block, sides, width):
    for axis, dim in sides:
        count = lax.axis_size(axis)
        forward = [(i, i + 1) for i in range(count - 1)]
        backward = [(target, source) for source, target in forward]
        low = lax.ppermute(
            lax.slice_in_dim(block, block.shape[dim] - width, None, axis=dim), axis, forward
        )
        high = lax.ppermute(lax.slice_in_dim(block, 0, width, axis=dim), axis, backward)
        block = jnp.concatenate([low, block, high], axis=dim)
    return block


def border_packet(field_now):
    return jnp.concatenate(
        [field_now[..., 0, :], field_now[..., -1, :], field_now[..., :, 0], field_now[..., :, -1]],
        -1,
    )


def panel_border_set(packets, row_count, tile_count):
    side_len = row_count * tile_count
    west_cols = packets[..., 2 * side_len : 2 * side_len + row_count]
    east_cols = packets[..., 2 * side_len + row_count :]
    west_line = jnp.moveaxis(west_cols, 0, 2).reshape(
        west_cols.shape[1], west_cols.shape[2], side_len
    )
    east_line = jnp.moveaxis(east_cols, 0, 2).reshape(
        east_cols.shape[1], east_cols.shape[2], side_len
    )
    north_line = packets[0, ..., :side_len]
    south_line = packets[tile_count - 1, ..., side_len : 2 * side_len]
    return jnp.stack([west_line, east_line, north_line, south_line], 0)


def transport(field_now, coefficients, padded):
    west_cells = padded[..., 1:-1, :-2]
    east_cells = padded[..., 1:-1, 2:]
    north_cells = padded[..., :-2, 1:-1]
    south_cells = padded[..., 2:, 1:-1]
    speed_x = coefficients[:, 0][:, None]
    speed_y = coefficients[:, 1][:, None]
    mixing = coefficients[:, 2][:, None]
    return (
        field_now
        - speed_x * (field_now - west_cells)
        - speed_y * (field_now - north_cells)
        + mixing * (west_cells + east_cells + north_cells + south_cells - 4.0 * field_now)
    )


def pool_blocks(block_values, block_weights):
    count, levels_here, tracer_count, _ = block_values.shape
    extra = 3 * WIN - BEDGE
    scaled = (block_values * block_weights[:, None, None, :]).reshape(
        count, levels_here, tracer_count, BEDGE, BEDGE
    )
    scaled = jnp.pad(scaled, ((0, 0), (0, 0), (0, 0), (0, extra), (0, extra)))
    mass_window = scaled.reshape(count, levels_here, tracer_count, WIN, 3, WIN, 3).sum((4, 6))
    spread = jnp.pad(block_weights.reshape(count, BEDGE, BEDGE), ((0, 0), (0, extra), (0, extra)))
    cover_window = spread.reshape(count, WIN, 3, WIN, 3).sum((2, 4))
    return (
        mass_window.reshape(count, levels_here, tracer_count, WIN * WIN),
        cover_window.reshape(count, WIN * WIN),
    )


def deposit_windows(totals, mass_window, cover_window, corners, first_row, row_count, side_len):
    owned = row_count * side_len
    corner_row = corners // side_len
    corner_col = corners % side_len
    offsets = jnp.arange(WIN, dtype=jnp.int32)
    rows_local = corner_row[:, None, None] + offsets[None, :, None] - first_row
    cols_here = corner_col[:, None, None] + offsets[None, None, :]
    inside = (rows_local >= 0) & (rows_local < row_count)
    target = jnp.where(inside, rows_local * side_len + cols_here, owned).reshape(-1)
    levels_here, tracer_count = (mass_window.shape[1], mass_window.shape[2])
    flat_mass = jnp.moveaxis(mass_window, 0, 2).reshape(levels_here, tracer_count, -1)
    mass_total = totals[0].at[:, :, target].add(flat_mass, mode="drop")
    cover_total = totals[1].at[target].add(cover_window.reshape(-1), mode="drop")
    return (mass_total, cover_total)


def body(parent, courant, edge_links, nest_tracer, nest_weight, nest_map, block_live):
    field_now = parent[0]
    levels_here, tracer_count, row_count, side_len = field_now.shape
    tile_count = lax.axis_size("tile")
    tile_pos = lax.axis_index("tile")
    panel_pos = lax.axis_index("panel")
    packet = border_packet(field_now)
    framed = extended(field_now, (("tile", 2),), 1)
    upper_row = framed[:, :, 0, :]
    lower_row = framed[:, :, -1, :]
    everyone = lax.all_gather(packet[None], ("panel", "tile"), axis=0, tiled=True)
    everyone = everyone.reshape((-1, tile_count) + everyone.shape[1:])
    borders = jax.vmap(lambda packets: panel_border_set(packets, row_count, tile_count))(everyone)
    links_here = edge_links[panel_pos]
    strips = []
    for border in range(4):
        partner = links_here[border]
        strip_line = borders[partner[0], partner[1]]
        strip_line = jnp.where(partner[2] == 1, jnp.flip(strip_line, -1), strip_line)
        strips.append(strip_line)
    start_row = tile_pos * row_count
    west_halo = lax.dynamic_slice_in_dim(strips[0], start_row, row_count, 2)
    east_halo = lax.dynamic_slice_in_dim(strips[1], start_row, row_count, 2)
    upper_row = jnp.where(tile_pos == 0, strips[2], upper_row)
    lower_row = jnp.where(tile_pos == tile_count - 1, strips[3], lower_row)
    middle = jnp.concatenate([upper_row[:, :, None, :], field_now, lower_row[:, :, None, :]], 2)
    corner = jnp.zeros((levels_here, tracer_count, 1), jnp.float32)
    west_column = jnp.concatenate([corner, west_halo, corner], 2)
    east_column = jnp.concatenate([corner, east_halo, corner], 2)
    padded = jnp.concatenate([west_column[..., None], middle, east_column[..., None]], 3)
    moved_field = transport(field_now, courant[0], padded)
    weights = nest_weight[0] * block_live[0][:, None].astype(jnp.float32)
    tracer_values = nest_tracer[0]
    cell_index = nest_map[0]
    owned = row_count * side_len
    start_value = (
        jnp.zeros((levels_here, tracer_count, owned), jnp.float32),
        jnp.zeros((owned,), jnp.float32),
    )
    piece_values = lax.all_gather(tracer_values, "tile", axis=0, tiled=True)
    piece_weights = lax.all_gather(weights, "tile", axis=0, tiled=True)
    piece_index = lax.all_gather(cell_index, "tile", axis=0, tiled=True)
    piece_mass, piece_cover = pool_blocks(piece_values, piece_weights)
    mass_here, cover_here = deposit_windows(
        start_value, piece_mass, piece_cover, piece_index[:, 0], start_row, row_count, side_len
    )
    blended = (moved_field + mass_here.reshape(levels_here, tracer_count, row_count, side_len)) / (
        1.0 + cover_here.reshape(row_count, side_len)
    )
    return blended[None]


def solution(mesh):
    placed = (
        P("panel", "lev", None, "tile", None),
        P("panel", "lev", None, "tile", None),
        P(),
        P("panel", "tile", "lev", None, None),
        P("panel", "tile", None),
        P("panel", "tile", None),
        P("panel", "tile"),
    )
    return jax.shard_map(
        body,
        mesh=mesh,
        in_specs=placed,
        out_specs=P("panel", "lev", None, "tile", None),
        check_vma=False,
    )
```

profile of v0, /device:TPU:1, one launch (start us, length us, event | category | flops | bytes accessed | tf_op | source)
XLA Modules:
  0.0 658.8 jit_solution(1350786356233825878)
XLA Ops:
  6.5 1.5 copy.88
  8.8 1.5 fusion.18
  10.4 1.1 copy.106
  11.8 0.7 concatenate.25
  13.1 16.2 %collective-permute-start = (f32[1,4,1,512]{3,1,2,0:T(4,128)S(1)}, f32[1,4,1,512]{3,1,2,0:T(4,128)S(1)}, u32[]{:S(2)}, u32[]{:S(2)}) collective-permute-start(f32[1,4,1,512]{3,1,2,0:T(4,128)S(1)} %get-tuple-element.9), channel_id=1, source_target_pairs={{0,8},{8,16},{16,24},{24,32},{32,40},{40,48},{48,56},{56,64},{64,7... | collective-permute-start | bytes 24584 | tf_op jit(solution)/shard_map/ppermute | solution.py:15
  29.4 1.9 collective-permute-start.1
  31.3 1.6 constant_dynamic-slice_fusion.6
  50.6 1.6 slice_bitcast_fusion.4
  52.2 40.1 %all-gather.11.cloned.1.call-done = s32[1,64,4096]{2,0,1:T(1,128)} async-done(((s32[1,4,4096]{2,0,1:T(1,128)}), s32[1,64,4096]{2,0,1:T(1,128)}) %all-gather.11.cloned.1.call-update) | async-done | bytes 1048592 | tf_op jit(solution)/shard_map/all_gather | solution.py:134
  92.3 1.8 copy.105
  94.9 1.1 select_n.140
  96.1 66.2 %all-gather.15.cloned.1.call-done = f32[16,4,4096]{2,1,0:T(4,128)} async-done(((f32[1,4,4096]{2,1,0:T(4,128)}), f32[16,4,4096]{2,1,0:T(4,128)}) %all-gather.15.cloned.1.call-update) | async-done | bytes 1048592 | tf_op jit(solution)/shard_map/all_gather | solution.py:133
  162.2 3.1 reshape.293
  165.3 2.4 copy.94
  167.7 1.7 pad.9
  169.4 3.0 reshape.294
  172.4 1.0 reduce_sum.19
  174.1 1.3 fusion.17
  175.4 166.0 %scatter_custom_fusion.1 = f32[16384]{0:T(1024)S(1)} fusion(s32[30976]{0:T(1024)S(1)} %fusion.17, f32[30976]{0:T(1024)S(1)} %reshape.309, f32[]{:T(128)} %constant.70.clone.1), kind=kCustom, calls=%fused_computation.44 | custom fusion | flops 30976 | bytes 65540 | tf_op jit(solution)/shard_map/scatter-add | solution.py:89
  341.4 1.6 reshape.320
  343.0 1.6 copy.81
  344.6 0.7 slice_bitcast_fusion.1
  345.3 1.0 reshape.322
  348.7 88.5 %all-gather.13.cloned.1.call-done = f32[1,64,1,4,4096]{4,3,2,0,1:T(4,128)} async-done(((f32[1,4,1,4,4096]{4,3,2,0,1:T(4,128)}), f32[1,64,1,4,4096]{4,3,2,0,1:T(4,128)}) %all-gather.13.cloned.1.call-update) | async-done | bytes 4194320 | tf_op jit(solution)/shard_map/all_gather | solution.py:132
  437.2 6.1 bitcast_multiply_fusion
  443.3 8.3 %copy.99 = f32[64,1,4,4096]{0,2,3,1:T(4,128)} copy(f32[64,1,4,4096]{3,2,0,1:T(4,128)} %bitcast_multiply_fusion) | data formatting | bytes 8388608 | tf_op jit(solution)/shard_map/reshape | solution.py:64
  451.6 8.6 %pad.8 = f32[64,1,4,66,66]{0,2,4,3,1:T(4,128)} pad(f32[64,1,4,64,64]{0,2,4,3,1:T(4,128)} %bitcast.97, f32[]{:T(128)} %constant.24.clone.1), padding=0_0x0_0x0_0x0_2x0_2 | pad | bytes 8654852 | tf_op jit(solution)/shard_map/jit(_pad)/pad | solution.py:67
  460.2 5.7 reduce_sum.18
  466.9 8.2 %copy.92 = f32[30976,4]{1,0:T(8,128)} copy(f32[30976,4]{0,1:T(4,128)S(1)} %bitcast.102) | data formatting | bytes 991232 | tf_op jit(solution)/shard_map/reshape | solution.py:87
  475.1 170.5 %scatter_custom_fusion = f32[4,16384]{0,1:T(8,128)} fusion(s32[30976]{0:T(1024)} %copy-done.3, f32[30976,4]{1,0:T(8,128)} %copy.92, f32[]{:T(128)} %constant.24.clone.1), kind=kCustom, calls=%fused_computation.3 | custom fusion | flops 123904 | bytes 262656 | tf_op jit(solution)/shard_map/scatter-add | solution.py:88
  645.6 5.3 copy.93
  651.5 0.8 copy.96
  (54 shorter events, 6.8 us)
Async XLA Ops:
  6.5 85.8 %all-gather.11.cloned.1.call-start = ((), (), s32[]{:S(2)}) async-start(), calls=%async_computation.1 | async-start | bytes 1114112 | tf_op jit(solution)/shard_map/all_gather | solution.py:134
  8.1 154.1 %all-gather.15.cloned.1.call-start = ((), (), s32[]{:S(2)}) async-start(), calls=%async_computation.3 | async-start | bytes 1114112 | tf_op jit(solution)/shard_map/all_gather | solution.py:133
  10.4 332.6 %all-gather.9.cloned.1.call-start = ((), (), s32[]{:S(2)}) async-start(), calls=%async_computation | async-start | bytes 1787904 | tf_op jit(solution)/shard_map/all_gather | solution.py:103
  12.6 424.6 %all-gather.13.cloned.1.call-start = ((), (), s32[]{:S(2)}) async-start(), calls=%async_computation.2 | async-start | bytes 4456448 | tf_op jit(solution)/shard_map/all_gather | solution.py:132
  13.1 335.6 %collective-permute-start = (f32[1,4,1,512]{3,1,2,0:T(4,128)S(1)}, f32[1,4,1,512]{3,1,2,0:T(4,128)S(1)}, u32[]{:S(2)}, u32[]{:S(2)}) collective-permute-start(f32[1,4,1,512]{3,1,2,0:T(4,128)S(1)} %get-tuple-element.9), channel_id=1, source_target_pairs={{0,8},{8,16},{16,24},{24,32},{32,40},{40,48},{48,56},{56,64},{64,7... | collective-permute-start | bytes 24584 | tf_op jit(solution)/shard_map/ppermute | solution.py:15
  29.4 318.6 %collective-permute-start.1 = (f32[1,4,1,512]{3,1,2,0:T(4,128)S(1)}, f32[1,4,1,512]{3,1,2,0:T(4,128)S(1)}, u32[]{:S(2)}, u32[]{:S(2)}) collective-permute-start(f32[1,4,1,512]{3,1,2,0:T(4,128)S(1)} %get-tuple-element.12), channel_id=1, source_target_pairs={{8,0},{16,8},{24,16},{32,24},{40,32},{48,40},{56,48},{64,56},{72,6... | collective-permute-start | bytes 24584 | tf_op jit(solution)/shard_map/ppermute | solution.py:18
  175.3 166.0 %copy-start.3 = (s32[30976]{0:T(1024)}, s32[30976]{0:T(1024)S(1)}, u32[]{:S(2)}) copy-start(s32[30976]{0:T(1024)S(1)} %fusion.17) | copy-start | bytes 371716
  645.6 5.3 copy-start
  645.6 5.4 copy-start.1
  645.6 5.4 copy-start.2
Sparse Core Ops, SparseCore 0:
  11.2 81.0 all-gather.10
  96.2 66.0 all-gather.14
  164.7 163.6 all-gather.8
  332.1 105.0 all-gather.12
where the time goes:
time: 660 us; the launch traced here: 659 us
  other arithmetic  354 us (54%)
  waiting for transfers between devices  195 us (30%)
  local copies, waits for them, and re-layouts  59.9 us (9%)
  between operations  31.1 us (5%)
  starting transfers between devices  18.3 us (3%)
    scatter-add x1, other arithmetic, deposit_windows(): mass_total = totals[0].at[:, :, target].add(flat_mass, mode='drop')  170 us
    scatter-add x1, other arithmetic, deposit_windows(): totals[1].at[target].add(cover_window.reshape(-1), mode='drop')  166 us
    all_gather x1, waiting for transfers between devices, body(): piece_values = lax.all_gather(tracer_values, 'tile', axis=0, tiled=True)  88.5 us
    all_gather x1, waiting for transfers between devices, body(): piece_weights = lax.all_gather(weights, 'tile', axis=0, tiled=True)  66.2 us
    all_gather x1, waiting for transfers between devices, body(): piece_index = lax.all_gather(cell_index, 'tile', axis=0, tiled=True)  40.1 us
    ppermute x1, starting transfers between devices, extended(): lax.ppermute(lax.slice_in_dim(block, block.shape[dim] - width, None, axis...  16.2 us
  transfers between devices with their start and end apart: 6, of which 3 were waited for; matrix products, arithmetic and copies ran while one was open for 30% of the time, Pallas kernels for 0%

commit v1 on v0

v1 whole, which is shorter than its diff:
```python
import functools

import jax
import jax.numpy as jnp
from jax import lax
from jax.experimental import pallas as pl
from jax.experimental.pallas import tpu as pltpu
from jax.sharding import PartitionSpec as P

WIN = 22
WROWS = 24
FAR = -(64 * 512)
ZROW = 4 * WROWS
ZMETA = ZROW + 16
ZALL = ZMETA + 8
GROWS = 2 * ZROW
GLINES = GROWS + 32
GMETA = GLINES + 64
GALL = GMETA + 8
VMEM = pl.BlockSpec(memory_space=pltpu.VMEM)
SMEM = pl.BlockSpec(memory_space=pltpu.SMEM)


def tile_of(x, z, c):
    return (x * 2 + z) * 2 + c


def place_of():
    t = lax.axis_index("tile")
    return t, t // 4, (t // 2) % 2, t % 2


def lane_rows(line):
    return jnp.concatenate([line[:, 128 * k : 128 * (k + 1)] for k in range(4)], 0)


def three(x):
    hi = x.astype(jnp.bfloat16)
    rest = x - hi.astype(jnp.float32)
    mid = rest.astype(jnp.bfloat16)
    low = (rest - mid.astype(jnp.float32)).astype(jnp.bfloat16)
    return hi, mid, low


def dot(a, b):
    return jnp.dot(a, b, preferred_element_type=jnp.float32)


def border_kernel(parent_ref, slot_ref, rows_ref):
    t, _, _, c = place_of()
    west = parent_ref[:, :, 0:128].reshape(128, 128).T[0:1]
    east = parent_ref[:, :, 384:512].reshape(128, 128).T[127:128]
    first = lane_rows(parent_ref[:, 0, :])
    last = lane_rows(parent_ref[:, 31, :])
    line = jnp.where(t == 0, first, last)
    packet = jnp.concatenate([west, east, jnp.zeros((6, 128), jnp.float32), line], 0)
    for k in range(12):
        slot_ref[k] = packet
    rows_ref[0:16] = jnp.where(c == 0, first, last)
    rows_ref[16:32] = jnp.where(c == 0, last, first)


def pool_kernel(x_ref, w_ref, map_ref, live_ref, rows_ref, out_ref):
    pieces = []
    for blk in range(4):
        live = live_ref[0, blk].astype(jnp.float32)
        weight = w_ref[pl.ds(blk, 32, stride=4), :] * live
        for m in range(4):
            pieces.append(x_ref[blk, pl.ds(m, 32, stride=4), :] * weight)
        pieces.append(weight)
    parts = jnp.concatenate(three(jnp.concatenate(pieces, 1)), 0)
    row = lax.broadcasted_iota(jnp.int32, (48, 96), 0)
    col = lax.broadcasted_iota(jnp.int32, (48, 96), 1)
    odd = (row >= WROWS).astype(jnp.int32)
    nest_row = 2 * (col & 31) + odd
    take = ((nest_row * 43) >> 7) == row - WROWS * odd
    halves = dot(take.astype(jnp.float32).astype(jnp.bfloat16), parts)
    lane = lax.broadcasted_iota(jnp.int32, (WROWS, halves.shape[1]), 1)
    pooled = jnp.where((lane & 64) == 0, halves[:WROWS], halves[WROWS:])
    pooled = jnp.concatenate([pooled[:, 640 * b : 640 * (b + 1)] for b in range(4)], 0)
    row = lax.broadcasted_iota(jnp.int32, (640, 128), 0)
    col = lax.broadcasted_iota(jnp.int32, (640, 128), 1)
    into = (row >> 7) * WIN + (((row & 63) * 43) >> 7)
    gather = (into == col).astype(jnp.float32).astype(jnp.bfloat16)
    hi, mid, low = three(pooled)
    out_ref[0:ZROW] = dot(hi, gather) + dot(mid, gather) + dot(low, gather)
    out_ref[ZROW:ZMETA] = rows_ref[0:16]
    lane = lax.broadcasted_iota(jnp.int32, (8, 128), 1)
    meta = jnp.full((8, 128), FAR, jnp.int32)
    for blk in range(4):
        corner = jnp.where(live_ref[0, blk] != 0, map_ref[blk : blk + 1, 0:1], FAR)
        meta = jnp.where(lane == blk, corner, meta)
    out_ref[ZMETA:ZALL] = meta.astype(jnp.float32)


def pack_kernel(own_ref, other_ref, slots_ref, rows_ref, links_ref, out_ref):
    _, x, _, c = place_of()
    panel = lax.axis_index("panel")
    out_ref[0:ZROW] = own_ref[0:ZROW]
    out_ref[ZROW:GROWS] = other_ref[0:ZROW]
    out_ref[GROWS : GROWS + 16] = rows_ref[16:32]
    out_ref[GROWS + 16 : GLINES] = other_ref[ZROW:ZMETA]
    lane = lax.broadcasted_iota(jnp.int32, (4, 128), 1)
    trc = lax.broadcasted_iota(jnp.int32, (4, 128), 0)
    part = lax.broadcasted_iota(jnp.int32, (16, 128), 0) >> 2
    for side in range(4):
        q = links_ref[panel, side, 0]
        r = links_ref[panel, side, 1]
        piece = jnp.zeros((4, 128), jnp.float32)
        for z in range(2):
            column = slots_ref[2 * q + z, pl.ds(r & 1, 1), :]
            start = 64 * z + 32 * c
            for m in range(4):
                turned = pltpu.roll(jnp.broadcast_to(column, (8, 128)), (start - 32 * m + 128) % 128, 1)[0:4]
                inside = (trc == m) & (lane >= start) & (lane < start + 32)
                piece = jnp.where(inside, turned, piece)
        column_lines = jnp.where(part == x, jnp.concatenate([piece] * 4, 0), 0.0)
        row_line = slots_ref[2 * q + (r & 1), 8:24, :]
        holds = ((r == 2) & (x == 0) & (c == 0)) | ((r == 3) & (x == 3) & (c == 1))
        row_lines = jnp.where(holds, row_line, 0.0)
        out_ref[GLINES + 16 * side : GLINES + 16 * (side + 1)] = jnp.where(r < 2, column_lines, row_lines)
    lane = lax.broadcasted_iota(jnp.int32, (8, 128), 1)
    out_ref[GMETA:GALL] = jnp.where(
        lane < 4, own_ref[ZMETA:ZALL], pltpu.roll(other_ref[ZMETA:ZALL], 4, 1)
    )


def final_kernel(near_ref, far_ref, parent_ref, courant_ref, links_ref, out_ref, total_ref, lines_ref, meta_ref, corner_ref, sem):
    t, x, z, c = place_of()
    panel = lax.axis_index("panel")
    refs = (near_ref, far_ref)
    for k in range(2):
        for s in range(4):
            meta_ref[4 * k + s : 4 * k + s + 1] = refs[k][s, GMETA : GMETA + 1]
    copy = pltpu.make_async_copy(meta_ref, corner_ref, sem)
    copy.start()
    total_ref[:, 16:56, :] = jnp.zeros((5, 40, 640), jnp.float32)

    lines = near_ref[0, GLINES:GMETA]
    for s in range(1, 4):
        lines = lines + near_ref[s, GLINES:GMETA]
    for s in range(4):
        lines = lines + far_ref[s, GLINES:GMETA]
    row = lax.broadcasted_iota(jnp.int32, (128, 128), 0)
    col = lax.broadcasted_iota(jnp.int32, (128, 128), 1)
    mirror = (row + col == 127).astype(jnp.float32).astype(jnp.bfloat16)
    hi, mid, low = three(lines)
    turned = dot(hi, mirror) + dot(mid, mirror) + dot(low, mirror)
    for side in range(4):
        for k in range(4):
            lines_ref[0, side, 4 * k : 4 * k + 4] = lines[16 * side + 4 * k : 16 * side + 4 * k + 4]
            back = 3 - k
            lines_ref[1, side, 4 * k : 4 * k + 4] = turned[16 * side + 4 * back : 16 * side + 4 * back + 4]

    def column_halo(side):
        flip = links_ref[panel, side, 2]
        piece = lines_ref[flip, side, pl.ds(4 * x, 4), :]
        piece = jnp.concatenate([piece, piece], 0)
        piece = pltpu.roll(piece, (128 - 32 * (t % 4)) % 128, 1)
        piece = jnp.concatenate([piece, jnp.zeros((120, 128), jnp.float32)], 0)
        return piece.T[0:32]

    west_halo = column_halo(0)
    east_halo = column_halo(1)
    north_line = lines_ref[links_ref[panel, 2, 2], 2]
    south_line = lines_ref[links_ref[panel, 3, 2], 3]
    kept = slice(GROWS, GROWS + 16)
    passed = slice(GROWS + 16, GLINES)
    before = near_ref if False else far_ref
    north_of_0 = far_ref[lax.rem(x + 3 + z, 4), passed, :]
    north_of_1 = far_ref[x, kept, :]
    north = jnp.where(c == 0, north_of_0, north_of_1)
    south_of_0 = far_ref[x, kept, :]
    south_of_1 = far_ref[lax.rem(x + z, 4), passed, :]
    south = jnp.where(c == 0, south_of_0, south_of_1)
    north = jnp.where(t == 0, north_line, north)
    south = jnp.where(t == 15, south_line, south)

    copy.wait()
    lane = lax.broadcasted_iota(jnp.int32, (32, 128), 1)
    sub = lax.broadcasted_iota(jnp.int32, (32, 128), 0)
    first_row = 32 * t
    for k in range(2):

        def deposit(i, carry, k=k):
            s = i // 8
            j = lax.rem(i, 8)
            corner = corner_ref[4 * k + s, j].astype(jnp.int32)
            r = (corner >> 9) - first_row

            @pl.when((r > -(WIN + 1)) & (r < 32))
            def _():
                b = corner & 511
                start = pl.multiple_of(j * WROWS, 8)
                window = refs[k][s, pl.ds(start, WROWS), :]
                window = jnp.concatenate([window, jnp.zeros((8, 128), jnp.float32)], 0)
                at = r + 24
                rows = pl.ds(pl.multiple_of((at >> 3) * 8, 8), 32)
                window = pltpu.roll(window, at & 7, 0)
                q = pl.multiple_of((b >> 7) * 128, 128)
                off = b & 127
                low_side = (lane >= off) & (lane < off + WIN)
                high_side = lane < off + WIN - 128
                for m in range(5):
                    moved = pltpu.roll(window, (off - WIN * m + 128) % 128, 1)
                    here = pl.ds(q, 128)
                    total_ref[m, rows, here] += jnp.where(low_side, moved, 0.0)
                    there = pl.ds(pl.multiple_of(q + 128, 128), 128)
                    total_ref[m, rows, there] += jnp.where(high_side, moved, 0.0)

            return carry

        lax.fori_loop(0, 32, deposit, 0)

    def deposited(m):
        mass = total_ref[m, 24:56, 0:512]
        spill = total_ref[m, 16:56, 512:640]
        spill = pltpu.roll(spill, 33, 0)[0:32]
        return jnp.concatenate([mass[:, 0:128] + spill, mass[:, 128:512]], 1)

    scale = 1.0 / (1.0 + deposited(4))
    u = courant_ref[0]
    v = courant_ref[1]
    mix = courant_ref[2]
    column = lax.broadcasted_iota(jnp.int32, (32, 512), 1)
    line = lax.broadcasted_iota(jnp.int32, (32, 512), 0)
    for m in range(4):
        here = parent_ref[m]
        west = jnp.where(column == 0, west_halo[:, m : m + 1], pltpu.roll(here, 1, 1))
        east = jnp.where(column == 511, east_halo[:, m : m + 1], pltpu.roll(here, 511, 1))
        north_row = jnp.concatenate([north[4 * k + m : 4 * k + m + 1] for k in range(4)], 1)
        south_row = jnp.concatenate([south[4 * k + m : 4 * k + m + 1] for k in range(4)], 1)
        up = jnp.where(line == 0, north_row, pltpu.roll(here, 1, 0))
        down = jnp.where(line == 31, south_row, pltpu.roll(here, 31, 0))
        moved = here - u * (here - west) - v * (here - up) + mix * (west + east + up + down - 4.0 * here)
        out_ref[m] = (moved + deposited(m)) * scale


def shape(*dims):
    return jax.ShapeDtypeStruct(dims, jnp.float32)


def body(parent, courant, edge_links, nest_tracer, nest_weight, nest_map, block_live):
    params = pltpu.CompilerParams(vmem_limit_bytes=32 * 1024 * 1024)
    parent = parent[0, 0]
    slots, rows = pl.pallas_call(
        border_kernel,
        out_shape=(shape(12, 24, 128), shape(32, 128)),
        in_specs=[VMEM],
        out_specs=(VMEM, VMEM),
        compiler_params=params,
    )(parent)
    lines_of_z = [
        [p * 16 + tile_of(x, z, c) for p in range(6) for z in range(2)] for x in range(4) for c in range(2)
    ]
    slots = lax.all_to_all(slots, ("panel", "tile"), 0, 0, tiled=True, axis_index_groups=lines_of_z)

    values = nest_tracer[0, :, 0].reshape(4, 4, 32, 128).transpose(0, 2, 1, 3).reshape(4, 128, 128)
    weights = nest_weight[0].reshape(4, 32, 128).transpose(1, 0, 2).reshape(128, 128)
    own = pl.pallas_call(
        pool_kernel,
        grid=(1,),
        out_shape=shape(ZALL, 128),
        in_specs=[
            VMEM,
            VMEM,
            pl.BlockSpec((4, 128), lambda i: (0, 0)),
            SMEM,
            VMEM,
        ],
        out_specs=VMEM,
        compiler_params=params,
    )(values, weights, nest_map[0], block_live, rows)
    other = lax.ppermute(own, "tile", [(t, t ^ 2) for t in range(16)])
    packed = pl.pallas_call(
        pack_kernel,
        out_shape=shape(GALL, 128),
        in_specs=[VMEM, VMEM, VMEM, VMEM, SMEM],
        out_specs=VMEM,
        compiler_params=params,
    )(own, other, slots, rows, edge_links)
    chips = [[tile_of(x, z, c) for x in range(4)] for z in range(2) for c in range(2)]
    near = lax.all_gather(packed, "tile", axis=0, axis_index_groups=chips)
    far = lax.ppermute(near, "tile", [(t, t ^ 1) for t in range(16)])
    out = pl.pallas_call(
        final_kernel,
        out_shape=shape(4, 32, 512),
        in_specs=[VMEM, VMEM, VMEM, VMEM, SMEM],
        out_specs=VMEM,
        scratch_shapes=[
            pltpu.VMEM((5, 88, 640), jnp.float32),
            pltpu.VMEM((2, 4, 16, 128), jnp.float32),
            pltpu.VMEM((8, 128), jnp.float32),
            pltpu.SMEM((8, 128), jnp.float32),
            pltpu.SemaphoreType.DMA,
        ],
        compiler_params=params,
    )(near, far, parent, courant[0, 0], edge_links)
    return out[None, None]


def solution(mesh):
    placed = (
        P("panel", "lev", None, "tile", None),
        P("panel", "lev", None, "tile", None),
        P(),
        P("panel", "tile", "lev", None, None),
        P("panel", "tile", None),
        P("panel", "tile", None),
        P("panel", "tile"),
    )
    return jax.shard_map(
        body,
        mesh=mesh,
        in_specs=placed,
        out_specs=P("panel", "lev", None, "tile", None),
        check_vma=False,
    )
```

time: 660 us -> 56.5 us (0.09)
  other arithmetic: 354 us -> 0 us
  waiting for transfers between devices: 195 us -> 4.91 us
  local copies, waits for them, and re-layouts: 59.9 us -> 1.71 us
  between operations: 31.1 us -> 0.09 us
  blocking collectives: 0 us -> 12.1 us
  starting transfers between devices: 18.3 us -> 29.6 us
  Pallas kernels: 0 us -> 7.69 us
    scatter-add x2 -> x0, other arithmetic: 336 us -> none  [the longest x1 170 us: deposit_windows(): mass_total = totals[0].at[:, :, target].add(flat_mass, mode='drop')]
    all_gather x4 -> x0, waiting for transfers between devices: 195 us -> none  [the longest x1 88.5 us: body(): piece_values = lax.all_gather(tracer_values, 'tile', axis=0, tiled=True)]
    reshape x11 -> x0, local copies, waits for them, and re-layouts: 32.2 us -> none  [the longest x2 8.82 us: deposit_windows(): jnp.moveaxis(mass_window, 0, 2).reshape(levels_here, tracer_count, -1)]
    all_to_all x0 -> x1, starting transfers between devices: none -> 15.8 us  [body(): lax.all_to_all(slots, ('panel', 'tile'), 0, 0, tiled=True, axis_index_gro...]
    all_gather x0 -> x1, blocking collectives: none -> 12.1 us  [body(): near = lax.all_gather(packed, 'tile', axis=0, axis_index_groups=chips)]
    pad x2 -> x0, local copies, waits for them, and re-layouts: 10.3 us -> none  [the longest x1 8.63 us: pool_blocks(): scaled = jnp.pad(scaled, ((0, 0), (0, 0), (0, 0), (0, extra), (0, extra)))]
    pallas_call x0 -> x4, Pallas kernels: none -> 7.69 us  [the longest x1 5.07 us: body(): pl.pallas_call(final_kernel, out_shape=shape(4, 32, 512), in_specs=[VMEM,...]
    reduce_sum x2 -> x0, other arithmetic: 6.74 us -> none  [the longest x1 5.73 us: pool_blocks(): scaled.reshape(count, levels_here, tracer_count, WIN, 3, WIN, 3).sum((4, 6))]
  transfers between devices with their start and end apart: 6 -> 3, of which waited for: 3 -> 2; matrix products, arithmetic and copies ran while one was open for 30% -> 0% of each run, Pallas kernels for 0% -> 2%
where the time goes in v1:
time: 56.5 us; the launch traced here: 56.1 us
  starting transfers between devices  29.6 us (52%)
  blocking collectives  12.1 us (21%)
  Pallas kernels  7.69 us (14%)
  waiting for transfers between devices  4.91 us (9%)
  local copies, waits for them, and re-layouts  1.71 us (3%)
    all_to_all x1, starting transfers between devices, body(): lax.all_to_all(slots, ('panel', 'tile'), 0, 0, tiled=True, axis_index_gro...  15.8 us
    all_gather x1, blocking collectives, body(): near = lax.all_gather(packed, 'tile', axis=0, axis_index_groups=chips)  12.1 us
    ppermute x1, starting transfers between devices, body(): other = lax.ppermute(own, 'tile', [(t, t ^ 2) for t in range(16)])  9.64 us
    pallas_call x1, Pallas kernels, body(): pl.pallas_call(final_kernel, out_shape=shape(4, 32, 512), in_specs=[VMEM,...  5.07 us
    ppermute x1, starting transfers between devices, body(): far = lax.ppermute(near, 'tile', [(t, t ^ 1) for t in range(16)])  4.12 us
    ppermute x1, waiting for transfers between devices, body(): other = lax.ppermute(own, 'tile', [(t, t ^ 2) for t in range(16)])  3.28 us
    unnamed x17, local copies, waits for them, and re-layouts  1.71 us
    ppermute x1, waiting for transfers between devices, body(): far = lax.ppermute(near, 'tile', [(t, t ^ 1) for t in range(16)])  1.63 us
  transfers between devices with their start and end apart: 3, of which 2 were waited for; matrix products, arithmetic and copies ran while one was open for 0% of the time, Pallas kernels for 2%

profile of v1, /device:TPU:1, one launch (start us, length us, event | category | flops | bytes accessed | tf_op | source)
XLA Modules:
  0.0 56.1 jit_solution(4155990173288657083)
XLA Ops:
  0.0 0.0 copy-start
  0.0 0.9 %copy-done = f32[1,1,4,32,512]{4,3,2,1,0:T(8,128)S(1)} copy-done((f32[1,1,4,32,512]{4,3,2,1,0:T(8,128)S(1)}, f32[1,1,4,32,512]{4,3,2,1,0:T(8,128)}, u32[]{:S(2)}) %copy-start) | copy-done | bytes 262168
  1.0 0.0 copy-start.2
  1.0 0.8 %shard_map.73 = (f32[12,24,128]{2,1,0:T(8,128)}, f32[32,128]{1,0:T(8,128)S(1)}) custom-call(f32[4,32,512]{2,1,0:T(8,128)S(1)} %bitcast.17), custom_call_target="tpu_custom_call" | custom-call | tf_op jit(solution)/shard_map/pallas_call | solution.py:246
  1.7 0.0 copy-start.4
  1.7 0.0 copy-start.5
  1.7 15.8 %all-to-all-start = ((f32[12,24,128]{2,1,0:T(8,128)}), f32[12,24,128]{2,1,0:T(8,128)S(1)}, u32[]{:S(2)}, u32[]{:S(2)}) async-start(f32[12,24,128]{2,1,0:T(8,128)} %get-tuple-element.8), calls=%async_computation | async-start | bytes 294912 | tf_op jit(solution)/shard_map/all_to_all | solution.py:256
  17.6 0.0 copy-start.6
  17.6 0.0 copy-done.2
  17.6 0.0 copy-done.4
  17.6 0.0 copy-done.5
  17.6 0.6 %copy-done.6 = s32[1,4]{1,0:T(1,128)S(1)} copy-done((s32[1,4]{1,0:T(1,128)S(1)}, s32[1,4]{1,0:T(1,128)}, u32[]{:S(2)}) %copy-start.6) | copy-done | bytes 40
  18.2 0.0 copy-start.7
  18.2 1.0 %shard_map.74.own_ref = f32[120,128]{1,0:T(8,128)S(1)} custom-call(f32[4,128,128]{2,1,0:T(8,128)S(1)} %bitcast.19, f32[128,128]{1,0:T(8,128)S(1)} %bitcast.21, s32[4,4096]{1,0:T(4,128)S(1)} %bitcast.22, s32[1,4]{1,0:T(1,128)S(1)} %copy-done.6, f32[32,128]{1,0:T(8,128)S(1)} %get-tuple-element.7.rows_ref), custom_call_target="tpu_custom_call" | custom-call | tf_op jit(solution)/shard_map/pallas_call | solution.py:260
  19.2 9.6 %collective-permute-start = (f32[120,128]{1,0:T(8,128)S(1)}, f32[120,128]{1,0:T(8,128)S(1)}, u32[]{:S(2)}, u32[]{:S(2)}) collective-permute-start(f32[120,128]{1,0:T(8,128)S(1)} %shard_map.74.own_ref), channel_id=1, source_target_pairs={{0,16},{8,24},{16,0},{24,8},{32,48},{40,56},{48,32},{56,40},{64,80... | collective-permute-start | bytes 184328 | tf_op jit(solution)/shard_map/ppermute | solution.py:274
  28.9 0.0 copy-done.7
  28.9 0.1 copy.10.links_ref
  29.0 3.3 %collective-permute-done.other_ref = f32[120,128]{1,0:T(8,128)S(1)} collective-permute-done((f32[120,128]{1,0:T(8,128)S(1)}, f32[120,128]{1,0:T(8,128)S(1)}, u32[]{:S(2)}, u32[]{:S(2)}) %collective-permute-start) | collective-permute-done | bytes 61472 | tf_op jit(solution)/shard_map/ppermute | solution.py:274
  32.3 0.0 all-to-all-done.slots_ref
  32.3 0.9 %shard_map.75 = f32[296,128]{1,0:T(8,128)S(1)} custom-call(f32[120,128]{1,0:T(8,128)S(1)} %shard_map.74.own_ref, f32[120,128]{1,0:T(8,128)S(1)} %collective-permute-done.other_ref, f32[12,24,128]{2,1,0:T(8,128)S(1)} %all-to-all-done.slots_ref, f32[32,128]{1,0:T(8,128)S(1)} %get-tuple-element.7.rows_ref, s32[6,4,3]{2,1,0:T(4,128)S(1)} %copy.10.links_ref), custom_call_target="tpu_custom_call" | custom-call | tf_op jit(solution)/shard_map/pallas_call | solution.py:275
  33.1 0.0 copy-start.1
  33.2 0.0 copy-start.3
  33.2 12.1 %all-gather = f32[1184,128]{1,0:T(8,128)S(1)} all-gather(f32[296,128]{1,0:T(8,128)S(1)} %shard_map.75), channel_id=2, replica_groups={{0,32,64,96},{8,40,72,104},{16,48,80,112},{24,56,88,120},{1,33,65,97},{..., dimensions={0}, use_global_device_ids=true | all-gather | bytes 757760 | tf_op jit(solution)/shard_map/all_gather | solution.py:283
  45.3 4.1 %collective-permute-start.1 = (f32[4,296,128]{2,1,0:T(8,128)S(1)}, f32[4,296,128]{2,1,0:T(8,128)S(1)}, u32[]{:S(2)}, u32[]{:S(2)}) collective-permute-start(f32[4,296,128]{2,1,0:T(8,128)S(1)} %bitcast.15), channel_id=1, source_target_pairs={{0,8},{8,0},{16,24},{24,16},{32,40},{40,32},{48,56},{56,48},{64,72... | collective-permute-start | bytes 1818632 | tf_op jit(solution)/shard_map/ppermute | solution.py:284
  49.4 1.6 %collective-permute-done.1.far_ref = f32[4,296,128]{2,1,0:T(8,128)S(1)} collective-permute-done((f32[4,296,128]{2,1,0:T(8,128)S(1)}, f32[4,296,128]{2,1,0:T(8,128)S(1)}, u32[]{:S(2)}, u32[]{:S(2)}) %collective-permute-start.1) | collective-permute-done | bytes 606240 | tf_op jit(solution)/shard_map/ppermute | solution.py:284
  51.1 0.0 copy-done.1
  51.1 0.0 copy-done.3
  51.1 5.1 %shard_map.76 = f32[4,32,512]{2,1,0:T(8,128)} custom-call(f32[4,296,128]{2,1,0:T(8,128)S(1)} %bitcast.16, f32[4,296,128]{2,1,0:T(8,128)S(1)} %collective-permute-done.1.far_ref, f32[4,32,512]{2,1,0:T(8,128)S(1)} %bitcast.18, f32[3,32,512]{2,1,0:T(8,128)S(1)} %bitcast.20, s32[6,4,3]{2,1,0:T(4,128)S(1)} %copy.10.links_ref), custom_call_target="tpu_custom_call" | custom-call | tf_op jit(solution)/shard_map/pallas_call | solution.py:285
Async XLA Ops:
  0.0 0.9 %copy-start = (f32[1,1,4,32,512]{4,3,2,1,0:T(8,128)S(1)}, f32[1,1,4,32,512]{4,3,2,1,0:T(8,128)}, u32[]{:S(2)}) copy-start(f32[1,1,4,32,512]{4,3,2,1,0:T(8,128)} %param.7) | copy-start | bytes 786436
  1.0 16.6 %copy-start.2 = (f32[1,4,1,4,4096]{4,3,2,1,0:T(4,128)S(1)}, f32[1,4,1,4,4096]{4,3,2,1,0:T(4,128)}, u32[]{:S(2)}) copy-start(f32[1,4,1,4,4096]{4,3,2,1,0:T(4,128)} %param.10) | copy-start | bytes 786436
  1.7 15.9 %copy-start.4 = (f32[1,4,4096]{2,1,0:T(4,128)S(1)}, f32[1,4,4096]{2,1,0:T(4,128)}, u32[]{:S(2)}) copy-start(f32[1,4,4096]{2,1,0:T(4,128)} %param.11) | copy-start | bytes 196612
  1.7 15.9 %copy-start.5 = (s32[1,4,4096]{2,1,0:T(4,128)S(1)}, s32[1,4,4096]{2,1,0:T(4,128)}, u32[]{:S(2)}) copy-start(s32[1,4,4096]{2,1,0:T(4,128)} %param.12) | copy-start | bytes 196612
  1.7 30.6 %all-to-all-start = ((f32[12,24,128]{2,1,0:T(8,128)}), f32[12,24,128]{2,1,0:T(8,128)S(1)}, u32[]{:S(2)}, u32[]{:S(2)}) async-start(f32[12,24,128]{2,1,0:T(8,128)} %get-tuple-element.8), calls=%async_computation | async-start | bytes 294912 | tf_op jit(solution)/shard_map/all_to_all | solution.py:256
  17.6 0.7 %copy-start.6 = (s32[1,4]{1,0:T(1,128)S(1)}, s32[1,4]{1,0:T(1,128)}, u32[]{:S(2)}) copy-start(s32[1,4]{1,0:T(1,128)} %live_ref.1) | copy-start | bytes 52
  18.2 10.6 %copy-start.7 = (s32[6,4,3]{0,1,2:T(4,128)S(1)}, s32[6,4,3]{0,1,2:T(4,128)}, u32[]{:S(2)}) copy-start(s32[6,4,3]{0,1,2:T(4,128)} %param.9) | copy-start | bytes 868
  19.2 13.0 %collective-permute-start = (f32[120,128]{1,0:T(8,128)S(1)}, f32[120,128]{1,0:T(8,128)S(1)}, u32[]{:S(2)}, u32[]{:S(2)}) collective-permute-start(f32[120,128]{1,0:T(8,128)S(1)} %shard_map.74.own_ref), channel_id=1, source_target_pairs={{0,16},{8,24},{16,0},{24,8},{32,48},{40,56},{48,32},{56,40},{64,80... | collective-permute-start | bytes 184328 | tf_op jit(solution)/shard_map/ppermute | solution.py:274
  33.1 17.9 %copy-start.1 = (f32[1,1,4,32,512]{4,3,2,1,0:T(8,128)S(1)}, f32[1,1,4,32,512]{4,3,2,1,0:T(8,128)}, u32[]{:S(2)}) copy-start(f32[1,1,4,32,512]{4,3,2,1,0:T(8,128)} %param.7) | copy-start | bytes 786436
  33.2 17.9 %copy-start.3 = (f32[1,1,3,32,512]{4,3,2,1,0:T(8,128)S(1)}, f32[1,1,3,32,512]{4,3,2,1,0:T(8,128)}, u32[]{:S(2)}) copy-start(f32[1,1,3,32,512]{4,3,2,1,0:T(8,128)} %param.8) | copy-start | bytes 589828
  45.3 5.8 %collective-permute-start.1 = (f32[4,296,128]{2,1,0:T(8,128)S(1)}, f32[4,296,128]{2,1,0:T(8,128)S(1)}, u32[]{:S(2)}, u32[]{:S(2)}) collective-permute-start(f32[4,296,128]{2,1,0:T(8,128)S(1)} %bitcast.15), channel_id=1, source_target_pairs={{0,8},{8,0},{16,24},{24,16},{32,40},{40,32},{48,56},{56,48},{64,72... | collective-permute-start | bytes 1818632 | tf_op jit(solution)/shard_map/ppermute | solution.py:284

commit v2 on v1

v2 whole, which is shorter than its diff:
```python
import jax
import jax.numpy as jnp
from jax import lax
from jax.experimental import pallas as pl
from jax.experimental.pallas import tpu as pltpu
from jax.sharding import PartitionSpec as P

WIN = 22
WROWS = 24
FAR = -(64 * 512)
OWN = 4 * WROWS
ZALL = OWN + 8
BOTH = 2 * OWN
SIDES = BOTH
KEPT = SIDES + 8
PASSED = KEPT + 16
SLOT = PASSED + 16
META = 112
VMEM = pl.BlockSpec(memory_space=pltpu.VMEM)
SMEM = pl.BlockSpec(memory_space=pltpu.SMEM)
ANY = pl.BlockSpec(memory_space=pl.ANY)


def tile_of(x, z, c):
    return (x * 2 + z) * 2 + c


def place_of():
    t = lax.axis_index("tile")
    return t, t // 4, (t // 2) % 2, t % 2


def lane_rows(line):
    return jnp.concatenate([line[:, 128 * k : 128 * (k + 1)] for k in range(4)], 0)


def three(x):
    hi = x.astype(jnp.bfloat16)
    rest = x - hi.astype(jnp.float32)
    mid = rest.astype(jnp.bfloat16)
    low = (rest - mid.astype(jnp.float32)).astype(jnp.bfloat16)
    return hi, mid, low


def dot(a, b):
    return jnp.dot(a, b, preferred_element_type=jnp.float32)


def dot_exact(a, picks):
    hi, mid, low = three(a)
    return dot(hi, picks) + dot(mid, picks) + dot(low, picks)


def picks_of(mask):
    return mask.astype(jnp.float32).astype(jnp.bfloat16)


def iota(dims, axis):
    return lax.broadcasted_iota(jnp.int32, dims, axis)


def pool_kernel(
    x_hbm, w_hbm, map_hbm, parent_hbm, live_hbm, out_ref, packet_ref, x_ref, w_ref, map_ref, live_ref, west_ref, east_ref, ends_ref, sems
):
    t, _, _, c = place_of()
    copies = [
        pltpu.make_async_copy(live_hbm, live_ref, sems.at[0]),
        pltpu.make_async_copy(w_hbm, w_ref, sems.at[1]),
        pltpu.make_async_copy(x_hbm, x_ref, sems.at[2]),
        pltpu.make_async_copy(map_hbm.at[:, 0:128], map_ref, sems.at[3]),
        pltpu.make_async_copy(parent_hbm.at[:, :, 0:128], west_ref, sems.at[4]),
        pltpu.make_async_copy(parent_hbm.at[:, :, 384:512], east_ref, sems.at[5]),
        pltpu.make_async_copy(parent_hbm.at[:, 0:8, :], ends_ref.at[0], sems.at[6]),
        pltpu.make_async_copy(parent_hbm.at[:, 24:32, :], ends_ref.at[1], sems.at[7]),
    ]
    for copy in copies:
        copy.start()
    row = iota((48, 96), 0)
    col = iota((48, 96), 1)
    odd = (row >= WROWS).astype(jnp.int32)
    nest_row = 2 * (col & 31) + odd
    take = picks_of(((nest_row * 43) >> 7) == row - WROWS * odd)
    row = iota((640, 128), 0)
    col = iota((640, 128), 1)
    gather = picks_of((row >> 7) * WIN + (((row & 63) * 43) >> 7) == col)
    for copy in copies[0:3]:
        copy.wait()
    pieces = []
    for blk in range(4):
        live = live_ref[0, blk].astype(jnp.float32)
        weight = w_ref[pl.ds(blk, 32, stride=4), :] * live
        for m in range(4):
            pieces.append(x_ref[blk, pl.ds(m, 32, stride=4), :] * weight)
        pieces.append(weight)
    parts = jnp.concatenate(three(jnp.concatenate(pieces, 1)), 0)
    halves = dot(take, parts)
    lane = iota((WROWS, halves.shape[1]), 1)
    pooled = jnp.where((lane & 64) == 0, halves[:WROWS], halves[WROWS:])
    pooled = jnp.concatenate([pooled[:, 640 * b : 640 * (b + 1)] for b in range(4)], 0)
    out_ref[0:OWN] = dot_exact(pooled, gather)
    for copy in copies[3:8]:
        copy.wait()
    lane = iota((1, 128), 1)
    meta = jnp.zeros((1, 128), jnp.int32)
    for blk in range(4):
        corner = jnp.where(live_ref[0, blk] != 0, map_ref[blk : blk + 1, 0:1], FAR)
        meta = jnp.where(lane == META + blk, corner, meta)
    out_ref[0:1] = jnp.where(lane < META, out_ref[0:1], meta.astype(jnp.float32))
    first = lane_rows(ends_ref[0, :, 0, :])
    last = lane_rows(ends_ref[1, :, 7, :])
    edge = jnp.where(c == 0, first, last)
    for b in range(4):
        out_ref[WROWS * b + WIN : WROWS * (b + 1)] = edge[2 * b : 2 * b + 2]
    out_ref[OWN:ZALL] = edge[8:16]
    west = west_ref[...].reshape(128, 128).T[0:1]
    east = east_ref[...].reshape(128, 128).T[127:128]
    line = jnp.where(t == 0, first, last)
    packet_ref[0:24] = jnp.concatenate([west, east, jnp.zeros((6, 128), jnp.float32), line], 0)
    packet_ref[24:40] = jnp.where(c == 0, last, first)


def border_kernel(packet_ref, slot_ref):
    for k in range(12):
        slot_ref[k] = packet_ref[0:24]


def inner_kernel(parent_ref, courant_ref, after_ref, out_ref):
    u = courant_ref[0]
    v = courant_ref[1]
    mix = courant_ref[2]
    column = iota((32, 512), 1)
    line = iota((32, 512), 0)
    for m in range(4):
        here = parent_ref[m]
        west = jnp.where(column == 0, 0.0, pltpu.roll(here, 1, 1))
        east = jnp.where(column == 511, 0.0, pltpu.roll(here, 511, 1))
        up = jnp.where(line == 0, 0.0, pltpu.roll(here, 1, 0))
        down = jnp.where(line == 31, 0.0, pltpu.roll(here, 31, 0))
        out_ref[m] = here - u * (here - west) - v * (here - up) + mix * (west + east + up + down - 4.0 * here)


def pack_kernel(own_ref, other_ref, slots_ref, links_ref, packet_ref, after_ref, out_ref):
    _, x, z, c = place_of()
    panel = lax.axis_index("panel")
    for s in range(4):
        out_ref[s, 0:OWN] = own_ref[0:OWN]
        out_ref[s, OWN:BOTH] = other_ref[0:OWN]
    passed = jnp.concatenate(
        [other_ref[WROWS * b + WIN : WROWS * (b + 1)] for b in range(4)] + [other_ref[OWN:ZALL]], 0
    )

    sides = (0, 1, 2 + z)
    links = [(links_ref[panel, s, 0], links_ref[panel, s, 1], links_ref[panel, s, 2]) for s in sides]
    halves = [(0, z ^ links[0][2]), (1, z ^ links[1][2]), (2, 0), (2, 1)]
    columns = []
    for k, half in halves:
        q, r, _ = links[k]
        columns.append(slots_ref[2 * q + half, pl.ds(r & 1, 1), :])
    columns = jnp.concatenate(columns + [jnp.zeros((4, 128), jnp.float32)], 0)
    near = iota((128, 128), 0)
    far = iota((128, 128), 1)
    back = dot_exact(columns, picks_of((near ^ 31) == far))
    columns = [jnp.where(links[k][2] == 1, back[i : i + 1], columns[i : i + 1]) for i, (k, _) in enumerate(halves)]
    lines = jnp.concatenate([slots_ref[2 * q + (r & 1), 8:24, :] for q, r, _ in links], 0)
    back = dot_exact(lines, picks_of((near ^ 127) == far))
    lines = [
        jnp.where(
            links[k][2] == 1,
            jnp.concatenate([back[16 * k + 4 * (3 - p) : 16 * k + 4 * (4 - p)] for p in range(4)], 0),
            lines[16 * k : 16 * (k + 1)],
        )
        for k in range(3)
    ]
    holds = [((r == 2) & (x == 0) & (c == 0)) | ((r == 3) & (x == 3) & (c == 1)) for _, r, _ in links]

    lane = iota((16, 128), 1)
    trc = iota((16, 128), 0) & 3
    part = iota((16, 128), 0) >> 2

    def spread(a):
        return a + pltpu.roll(a, 32, 1) + pltpu.roll(a, 64, 1) + pltpu.roll(a, 96, 1)

    for k in range(2):
        q, r, f = links[k]
        to_chip = jnp.where(f == 1, 3 - x, x)
        to_core = jnp.where(f == 1, 1 - c, c)
        for core in range(2):
            group = 2 * z + core
            cut = jnp.where((lane >> 5) == group, lines[k], 0.0)
            cut = jnp.where((lane >> 5) == trc, spread(cut), 0.0)
            cut = cut + pltpu.roll(cut, 15, 0) + pltpu.roll(cut, 14, 0) + pltpu.roll(cut, 13, 0)
            for s in range(4):
                from_column = jnp.where((to_chip == s) & (to_core == core), columns[k], 0.0)
                from_line = jnp.where(holds[k], cut[4 * s : 4 * s + 1], 0.0)
                at = SIDES + 2 * k + core
                out_ref[s, at : at + 1] = jnp.where(r < 2, from_column, from_line)

    q, r, f = links[2]
    to_chip = jnp.where(f == 1, 3 - x, x)
    ends = jnp.zeros((16, 128), jnp.float32)
    for half in range(2):
        group = jnp.where(f == 1, 3 - (2 * half + c), 2 * half + c)
        piece = jnp.broadcast_to(columns[2 + half], (16, 128))
        piece = spread(jnp.where((lane >> 5) == trc, piece, 0.0))
        ends = jnp.where(((lane >> 5) == group) & (part == to_chip), piece, ends)
    ends = jnp.where(r < 2, ends, jnp.where(holds[2], lines[2], 0.0))
    end_chip = 3 * z
    next_chip = jnp.where(z == 0, x + 1, x - 1)
    for s in range(4):
        rows = jnp.where((next_chip == s) & (c != z), passed, 0.0)
        rows = jnp.where(end_chip == s, ends, rows)
        for j in range(8):
            out_ref[s, WROWS * j + WIN : WROWS * (j + 1)] = rows[2 * j : 2 * j + 2]
    out_ref[x, PASSED:SLOT] = passed
    out_ref[x, KEPT:PASSED] = packet_ref[24:40]


def deposit(slot_ref, total_ref, meta_ref, corner_ref, list_ref, sem):
    t = lax.axis_index("tile")
    first_row = 32 * t
    meta = jnp.concatenate([slot_ref[i // 2, OWN * (i % 2) : OWN * (i % 2) + 1, :] for i in range(8)], 0)
    meta = meta.astype(jnp.int32)
    r = (meta >> 9) - first_row
    meta_ref[...] = jnp.where((r > -(WIN + 1)) & (r < 32), meta, -1)
    copy = pltpu.make_async_copy(meta_ref, corner_ref, sem)
    copy.start()
    total_ref[:, 16:56, :] = jnp.zeros((5, 40, 640), jnp.float32)
    copy.wait()
    count = jnp.int32(0)
    for i in range(32):
        corner = corner_ref[i // 4, META + i % 4]
        list_ref[0, count] = corner
        list_ref[1, count] = i
        count = count + jnp.where(corner >= 0, 1, 0)
    lane = iota((32, 128), 1)
    sub = iota((32, 128), 0)

    def one(n, carry):
        corner = list_ref[0, n]
        i = list_ref[1, n]
        at = (corner >> 9) - first_row + 24
        b = corner & 511
        off = b & 127
        turn = at & 7
        window = slot_ref[i >> 3, pl.ds(pl.multiple_of((i & 7) * WROWS, 8), WROWS), :]
        window = jnp.concatenate([window, jnp.zeros((8, 128), jnp.float32)], 0)
        window = pltpu.roll(window, turn, 0)
        rows = pl.ds(pl.multiple_of((at >> 3) * 8, 8), 32)
        q = (b >> 7) * 128
        here = pl.ds(pl.multiple_of(q, 128), 128)
        there = pl.ds(pl.multiple_of(q + 128, 128), 128)
        inside = (sub >= turn) & (sub < turn + WIN)
        low_side = inside & (lane >= off) & (lane < off + WIN)
        high_side = inside & (lane < off + WIN - 128)
        for m in range(5):
            moved = pltpu.roll(window, (off - WIN * m + 128) % 128, 1)
            total_ref[m, rows, here] += jnp.where(low_side, moved, 0.0)
            total_ref[m, rows, there] += jnp.where(high_side, moved, 0.0)
        return carry

    lax.fori_loop(0, count, one, 0)


def deposited(total_ref, m):
    mass = total_ref[m, 24:56, 0:512]
    spill = pltpu.roll(total_ref[m, 16:56, 512:640], 33, 0)[0:32]
    return jnp.concatenate([mass[:, 0:128] + spill, mass[:, 128:512]], 1)


def halo_sum(slot_ref):
    total = slot_ref[0, SIDES:KEPT]
    ends = None
    for s in range(4):
        rows = jnp.concatenate([slot_ref[s, WROWS * j + WIN : WROWS * (j + 1), :] for j in range(8)], 0)
        ends = rows if s == 0 else ends + rows
        total = total if s == 0 else total + slot_ref[s, SIDES:KEPT]
    return jnp.concatenate([total, ends], 0)


def near_kernel(slot_ref, inner_ref, out_ref, halo_ref, total_ref, meta_ref, corner_ref, list_ref, sem):
    deposit(slot_ref, total_ref, meta_ref, corner_ref, list_ref, sem)
    for m in range(4):
        out_ref[m] = inner_ref[m] + deposited(total_ref, m)
    out_ref[4] = 1.0 + deposited(total_ref, 4)
    halo_ref[...] = halo_sum(slot_ref)


def final_kernel(slot_ref, near_ref, halo_ref, courant_ref, out_ref, total_ref, meta_ref, corner_ref, list_ref, sem):
    _, x, z, c = place_of()
    halo = halo_ref[...] + halo_sum(slot_ref)
    ends = halo[8:24]
    kept = slot_ref[x, KEPT:PASSED]
    passed = slot_ref[x, PASSED:SLOT]
    north = jnp.where(c == 1, kept, jnp.where(z == 0, ends, passed))
    south = jnp.where(c == 0, kept, jnp.where(z == 0, passed, ends))
    west = jnp.where(c == 0, halo[0:1], halo[1:2])
    east = jnp.where(c == 0, halo[2:3], halo[3:4])
    west = jnp.broadcast_to(west, (128, 128)).T
    east = jnp.broadcast_to(east, (128, 128)).T
    deposit(slot_ref, total_ref, meta_ref, corner_ref, list_ref, sem)
    u = courant_ref[0]
    v = courant_ref[1]
    mix = courant_ref[2]
    lane = iota((32, 128), 1)
    first = jnp.where(lane == 0, u[:, 0:128] + mix[:, 0:128], 0.0)
    last = jnp.where(lane == 127, mix[:, 384:512], 0.0)
    line = iota((32, 512), 0)
    above = jnp.where(line == 0, v + mix, 0.0)
    below = jnp.where(line == 31, mix, 0.0)
    scale = 1.0 / (near_ref[4] + deposited(total_ref, 4))
    for m in range(4):
        value = near_ref[m] + deposited(total_ref, m)
        north_row = jnp.concatenate([north[4 * k + m : 4 * k + m + 1] for k in range(4)], 1)
        south_row = jnp.concatenate([south[4 * k + m : 4 * k + m + 1] for k in range(4)], 1)
        value = value + above * north_row + below * south_row
        left = value[:, 0:128] + first * west[32 * m : 32 * m + 32]
        right = value[:, 384:512] + last * east[32 * m : 32 * m + 32]
        out_ref[m] = jnp.concatenate([left, value[:, 128:384], right], 1) * scale


def shape(*dims):
    return jax.ShapeDtypeStruct(dims, jnp.float32)


def dma(n):
    return pltpu.SemaphoreType.DMA((n,))


def cost(bytes_accessed):
    return pl.CostEstimate(flops=bytes_accessed, bytes_accessed=bytes_accessed, transcendentals=0)


def body(parent, courant, edge_links, nest_tracer, nest_weight, nest_map, block_live):
    params = pltpu.CompilerParams(vmem_limit_bytes=32 * 1024 * 1024)
    parent = parent[0, 0]
    courant = courant[0, 0]
    values = nest_tracer[0, :, 0].reshape(4, 4, 32, 128).transpose(0, 2, 1, 3).reshape(4, 128, 128)
    weights = nest_weight[0].reshape(4, 32, 128).transpose(1, 0, 2).reshape(128, 128)
    own, packet = pl.pallas_call(
        pool_kernel,
        out_shape=(shape(ZALL, 128), shape(40, 128)),
        in_specs=[ANY] * 5,
        out_specs=(VMEM, VMEM),
        scratch_shapes=[
            pltpu.VMEM((4, 128, 128), jnp.float32),
            pltpu.VMEM((128, 128), jnp.float32),
            pltpu.VMEM((4, 128), jnp.int32),
            pltpu.SMEM((1, 4), jnp.int32),
            pltpu.VMEM((4, 32, 128), jnp.float32),
            pltpu.VMEM((4, 32, 128), jnp.float32),
            pltpu.VMEM((2, 4, 8, 512), jnp.float32),
            dma(8),
        ],
        compiler_params=params,
    )(*[pltpu.with_memory_space_constraint(a, pltpu.HBM) for a in (values, weights, nest_map[0], parent, block_live)])
    other = lax.ppermute(own, "tile", [(t, t ^ 2) for t in range(16)])
    slots = pl.pallas_call(
        border_kernel,
        out_shape=shape(12, 24, 128),
        in_specs=[VMEM],
        out_specs=VMEM,
        compiler_params=params,
    )(packet)
    lines_of_z = [
        [p * 16 + tile_of(x, z, c) for p in range(6) for z in range(2)] for x in range(4) for c in range(2)
    ]
    slots = lax.all_to_all(slots, ("panel", "tile"), 0, 0, tiled=True, axis_index_groups=lines_of_z)
    inner = pl.pallas_call(
        inner_kernel,
        out_shape=shape(4, 32, 512),
        in_specs=[VMEM, VMEM, ANY],
        out_specs=VMEM,
        compiler_params=params,
        cost_estimate=cost(1 << 24),
    )(parent, courant, other)
    packed = pl.pallas_call(
        pack_kernel,
        out_shape=shape(4, SLOT, 128),
        in_specs=[VMEM, VMEM, VMEM, SMEM, VMEM, ANY],
        out_specs=VMEM,
        compiler_params=params,
    )(own, other, slots, edge_links, packet, inner)
    chips = [[tile_of(x, z, c) for x in range(4)] for z in range(2) for c in range(2)]
    near = lax.all_to_all(packed, "tile", 0, 0, tiled=True, axis_index_groups=chips)
    far = lax.ppermute(near, "tile", [(t, t ^ 1) for t in range(16)])
    scratch = [
        pltpu.VMEM((5, 88, 640), jnp.float32),
        pltpu.VMEM((8, 128), jnp.int32),
        pltpu.SMEM((8, 128), jnp.int32),
        pltpu.SMEM((2, 40), jnp.int32),
        pltpu.SemaphoreType.DMA,
    ]
    summed, halo = pl.pallas_call(
        near_kernel,
        out_shape=(shape(5, 32, 512), shape(24, 128)),
        in_specs=[VMEM, VMEM],
        out_specs=(VMEM, VMEM),
        scratch_shapes=scratch,
        compiler_params=params,
        cost_estimate=cost(1 << 20),
    )(near, inner)
    out = pl.pallas_call(
        final_kernel,
        out_shape=shape(4, 32, 512),
        in_specs=[VMEM, VMEM, VMEM, VMEM],
        out_specs=VMEM,
        scratch_shapes=scratch,
        compiler_params=params,
    )(far, summed, halo, courant)
    return out[None, None]


def solution(mesh):
    placed = (
        P("panel", "lev", None, "tile", None),
        P("panel", "lev", None, "tile", None),
        P(),
        P("panel", "tile", "lev", None, None),
        P("panel", "tile", None),
        P("panel", "tile", None),
        P("panel", "tile"),
    )
    return jax.shard_map(
        body,
        mesh=mesh,
        in_specs=placed,
        out_specs=P("panel", "lev", None, "tile", None),
        check_vma=False,
    )
```

time: 56.5 us -> 53.3 us (0.943)
  local copies, waits for them, and re-layouts: 1.71 us -> 0.12 us
  blocking collectives: 12.1 us -> 10.8 us
  Pallas kernels: 7.69 us -> 6.58 us
  starting transfers between devices: 29.6 us -> 30.3 us
    all_gather x1 -> x0, blocking collectives: 12.1 us -> none  [body(): near = lax.all_gather(packed, 'tile', axis=0, axis_index_groups=chips)]
    all_to_all x0 -> x1, blocking collectives: none -> 10.8 us  [body(): lax.all_to_all(packed, 'tile', 0, 0, tiled=True, axis_index_groups=chips)]
    pallas_call x1, Pallas kernels: 5.07 us -> 1.81 us  [body(): pl.pallas_call(final_kernel, out_shape=shape(4, 32, 512), in_specs=[VMEM,...]
    pallas_call x3 -> x5, Pallas kernels: 2.62 us -> 4.77 us  [the longest x1 1.66 us: body(): pl.pallas_call(pool_kernel, out_shape=(shape(ZALL, 128), shape(40, 128)),...]
    ppermute x1, waiting for transfers between devices: 3.28 us -> 4.88 us  [body(): other = lax.ppermute(own, 'tile', [(t, t ^ 2) for t in range(16)])]
    unnamed x17 -> x7, local copies, waits for them, and re-layouts: 1.71 us -> 0.12 us
    ppermute x1, waiting for transfers between devices: 1.63 us -> 0.26 us  [body(): far = lax.ppermute(near, 'tile', [(t, t ^ 1) for t in range(16)])]
    ppermute x1, starting transfers between devices: 4.12 us -> 4.79 us  [body(): far = lax.ppermute(near, 'tile', [(t, t ^ 1) for t in range(16)])]
  transfers between devices with their start and end apart: 3 -> 3, of which waited for: 2 -> 2; matrix products, arithmetic and copies ran while one was open for 0% -> 0% of each run, Pallas kernels for 2% -> 3%
where the time goes in v2:
time: 53.3 us; the launch traced here: 53 us
  starting transfers between devices  30.3 us (57%)
  blocking collectives  10.8 us (20%)
  Pallas kernels  6.58 us (12%)
  waiting for transfers between devices  5.14 us (10%)
    all_to_all x1, starting transfers between devices, body(): lax.all_to_all(slots, ('panel', 'tile'), 0, 0, tiled=True, axis_index_gro...  15.8 us
    all_to_all x1, blocking collectives, body(): lax.all_to_all(packed, 'tile', 0, 0, tiled=True, axis_index_groups=chips)  10.8 us
    ppermute x1, starting transfers between devices, body(): other = lax.ppermute(own, 'tile', [(t, t ^ 2) for t in range(16)])  9.63 us
    ppermute x1, waiting for transfers between devices, body(): other = lax.ppermute(own, 'tile', [(t, t ^ 2) for t in range(16)])  4.88 us
    ppermute x1, starting transfers between devices, body(): far = lax.ppermute(near, 'tile', [(t, t ^ 1) for t in range(16)])  4.79 us
    pallas_call x1, Pallas kernels, body(): pl.pallas_call(final_kernel, out_shape=shape(4, 32, 512), in_specs=[VMEM,...  1.81 us
    pallas_call x1, Pallas kernels, body(): pl.pallas_call(pool_kernel, out_shape=(shape(ZALL, 128), shape(40, 128)),...  1.66 us
    pallas_call x1, Pallas kernels, body(): pl.pallas_call(near_kernel, out_shape=(shape(5, 32, 512), shape(24, 128))...  1.17 us
  transfers between devices with their start and end apart: 3, of which 2 were waited for; matrix products, arithmetic and copies ran while one was open for 0% of the time, Pallas kernels for 3%

profile of v2, /device:TPU:1, one launch (start us, length us, event | category | flops | bytes accessed | tf_op | source)
XLA Modules:
  0.0 53.0 jit_solution(2953945118265759258)
XLA Ops:
  0.0 1.7 %shard_map.73 = (f32[104,128]{1,0:T(8,128)S(1)}, f32[40,128]{1,0:T(8,128)S(1)}) custom-call(f32[4,128,128]{2,1,0:T(8,128)} %bitcast.18, f32[128,128]{1,0:T(8,128)} %bitcast.19, s32[4,4096]{1,0:T(4,128)} %bitcast.20, f32[4,32,512]{2,1,0:T(8,128)} %bitcast.14, s32[1,4]{1,0:T(1,128)} %live_hbm.1), custom_call_target="tpu_custom_call" | custom-call | tf_op jit(solution)/shard_map/pallas_call | solution.py:339
  1.7 0.0 copy-start
  1.7 0.7 %shard_map.74 = f32[12,24,128]{2,1,0:T(8,128)} custom-call(f32[40,128]{1,0:T(8,128)S(1)} %get-tuple-element.10.packet_ref), custom_call_target="tpu_custom_call" | custom-call | tf_op jit(solution)/shard_map/pallas_call | solution.py:357
  2.4 0.0 copy-start.2
  2.4 0.0 copy-start.1
  2.4 15.8 %all-to-all-start = ((f32[12,24,128]{2,1,0:T(8,128)}), f32[12,24,128]{2,1,0:T(8,128)S(1)}, u32[]{:S(2)}, u32[]{:S(2)}) async-start(f32[12,24,128]{2,1,0:T(8,128)} %shard_map.74), calls=%async_computation | async-start | bytes 294912 | tf_op jit(solution)/shard_map/all_to_all | solution.py:367
  18.2 9.6 %collective-permute-start = (f32[104,128]{1,0:T(8,128)S(1)}, f32[104,128]{1,0:T(8,128)S(1)}, u32[]{:S(2)}, u32[]{:S(2)}) collective-permute-start(f32[104,128]{1,0:T(8,128)S(1)} %get-tuple-element.9.own_ref), channel_id=1, source_target_pairs={{0,16},{8,24},{16,0},{24,8},{32,48},{40,56},{48,32},{56,40},{64,80... | collective-permute-start | bytes 159752 | tf_op jit(solution)/shard_map/ppermute | solution.py:356
  27.8 0.0 copy-done.2
  27.8 0.1 copy.10.links_ref
  28.0 4.9 %collective-permute-done.after_ref.other_ref = f32[104,128]{1,0:T(8,128)S(1)} collective-permute-done((f32[104,128]{1,0:T(8,128)S(1)}, f32[104,128]{1,0:T(8,128)S(1)}, u32[]{:S(2)}, u32[]{:S(2)}) %collective-permute-start) | collective-permute-done | bytes 53280 | tf_op jit(solution)/shard_map/ppermute | solution.py:356
  32.8 0.0 copy-done
  32.8 0.0 copy-done.1
  32.8 0.2 shard_map.75.after_ref.inner_ref
  33.1 0.0 all-to-all-done.slots_ref
  33.1 1.0 %shard_map.76 = f32[4,232,128]{2,1,0:T(8,128)S(1)} custom-call(f32[104,128]{1,0:T(8,128)S(1)} %get-tuple-element.9.own_ref, f32[104,128]{1,0:T(8,128)S(1)} %collective-permute-done.after_ref.other_ref, f32[12,24,128]{2,1,0:T(8,128)S(1)} %all-to-all-done.slots_ref, s32[6,4,3]{2,1,0:T(4,128)S(1)} %copy.10.links_ref, ...), custom_call_target="tpu_custom_call" | custom-call | tf_op jit(solution)/shard_map/pallas_call | solution.py:376
  34.1 10.8 %all_to_all.10.slot_ref = f32[4,232,128]{2,1,0:T(8,128)S(1)} all-to-all(f32[4,232,128]{2,1,0:T(8,128)S(1)} %shard_map.76), channel_id=1, replica_groups={{0,32,64,96},{8,40,72,104},{16,48,80,112},{24,56,88,120},{1,33,65,97},{..., dimensions={0} | all-to-all | bytes 950272 | tf_op jit(solution)/shard_map/all_to_all | solution.py:384
  45.0 4.8 %collective-permute-start.1 = (f32[4,232,128]{2,1,0:T(8,128)S(1)}, f32[4,232,128]{2,1,0:T(8,128)S(1)}, u32[]{:S(2)}, u32[]{:S(2)}) collective-permute-start(f32[4,232,128]{2,1,0:T(8,128)S(1)} %all_to_all.10.slot_ref), channel_id=1, source_target_pairs={{0,8},{8,0},{16,24},{24,16},{32,40},{40,32},{48,56},{56,48},{64,72... | collective-permute-start | bytes 1425416 | tf_op jit(solution)/shard_map/ppermute | solution.py:385
  49.8 1.2 %shard_map.77 = (f32[5,32,512]{2,1,0:T(8,128)S(1)}, f32[24,128]{1,0:T(8,128)S(1)}) custom-call(f32[4,232,128]{2,1,0:T(8,128)S(1)} %all_to_all.10.slot_ref, f32[4,32,512]{2,1,0:T(8,128)S(1)} %shard_map.75.after_ref.inner_ref), custom_call_target="tpu_custom_call" | custom-call | flops 1048576 | bytes 1048576 | tf_op jit(solution)/shard_map/pallas_call | solution.py:393
  50.9 0.3 collective-permute-done.1.slot_ref
  51.2 1.8 %shard_map.78 = f32[4,32,512]{2,1,0:T(8,128)} custom-call(f32[4,232,128]{2,1,0:T(8,128)S(1)} %collective-permute-done.1.slot_ref, f32[5,32,512]{2,1,0:T(8,128)S(1)} %get-tuple-element.11.near_ref, f32[24,128]{1,0:T(8,128)S(1)} %get-tuple-element.12.halo_ref, f32[3,32,512]{2,1,0:T(8,128)S(1)} %bitcast.17), custom_call_target="tpu_custom_call" | custom-call | tf_op jit(solution)/shard_map/pallas_call | solution.py:402
Async XLA Ops:
  1.7 31.2 %copy-start = (f32[1,1,4,32,512]{4,3,2,1,0:T(8,128)S(1)}, f32[1,1,4,32,512]{4,3,2,1,0:T(8,128)}, u32[]{:S(2)}) copy-start(f32[1,1,4,32,512]{4,3,2,1,0:T(8,128)} %param.7) | copy-start | bytes 786436
  2.4 25.5 %copy-start.2 = (s32[6,4,3]{0,1,2:T(4,128)S(1)}, s32[6,4,3]{0,1,2:T(4,128)}, u32[]{:S(2)}) copy-start(s32[6,4,3]{0,1,2:T(4,128)} %param.9) | copy-start | bytes 868
  2.4 30.5 %copy-start.1 = (f32[1,1,3,32,512]{4,3,2,1,0:T(8,128)S(1)}, f32[1,1,3,32,512]{4,3,2,1,0:T(8,128)}, u32[]{:S(2)}) copy-start(f32[1,1,3,32,512]{4,3,2,1,0:T(8,128)} %param.8) | copy-start | bytes 589828
  2.4 30.7 %all-to-all-start = ((f32[12,24,128]{2,1,0:T(8,128)}), f32[12,24,128]{2,1,0:T(8,128)S(1)}, u32[]{:S(2)}, u32[]{:S(2)}) async-start(f32[12,24,128]{2,1,0:T(8,128)} %shard_map.74), calls=%async_computation | async-start | bytes 294912 | tf_op jit(solution)/shard_map/all_to_all | solution.py:367
  18.2 14.6 %collective-permute-start = (f32[104,128]{1,0:T(8,128)S(1)}, f32[104,128]{1,0:T(8,128)S(1)}, u32[]{:S(2)}, u32[]{:S(2)}) collective-permute-start(f32[104,128]{1,0:T(8,128)S(1)} %get-tuple-element.9.own_ref), channel_id=1, source_target_pairs={{0,16},{8,24},{16,0},{24,8},{32,48},{40,56},{48,32},{56,40},{64,80... | collective-permute-start | bytes 159752 | tf_op jit(solution)/shard_map/ppermute | solution.py:356
  45.0 6.2 %collective-permute-start.1 = (f32[4,232,128]{2,1,0:T(8,128)S(1)}, f32[4,232,128]{2,1,0:T(8,128)S(1)}, u32[]{:S(2)}, u32[]{:S(2)}) collective-permute-start(f32[4,232,128]{2,1,0:T(8,128)S(1)} %all_to_all.10.slot_ref), channel_id=1, source_target_pairs={{0,8},{8,0},{16,24},{24,16},{32,40},{40,32},{48,56},{56,48},{64,72... | collective-permute-start | bytes 1425416 | tf_op jit(solution)/shard_map/ppermute | solution.py:385

commit v3 on v2

--- a/solution.py
+++ b/solution.py
@@ -16,6 +16,8 @@
 PASSED = KEPT + 16
 SLOT = PASSED + 16
 META = 112
+LEAD = 10
+XLEAD = 2
 VMEM = pl.BlockSpec(memory_space=pltpu.VMEM)
 SMEM = pl.BlockSpec(memory_space=pltpu.SMEM)
 ANY = pl.BlockSpec(memory_space=pl.ANY)
@@ -60,21 +62,42 @@
 
 
 def pool_kernel(
-    x_hbm, w_hbm, map_hbm, parent_hbm, live_hbm, out_ref, packet_ref, x_ref, w_ref, map_ref, live_ref, west_ref, east_ref, ends_ref, sems
+    x_hbm, w_hbm, map_hbm, parent_hbm, live_hbm, out_ref, slot_hbm, kept_ref,
+    x_ref, w_ref, map_ref, live_ref, west_ref, east_ref, ends_ref, packet_ref, sems
 ):
     t, _, _, c = place_of()
     copies = [
-        pltpu.make_async_copy(live_hbm, live_ref, sems.at[0]),
-        pltpu.make_async_copy(w_hbm, w_ref, sems.at[1]),
-        pltpu.make_async_copy(x_hbm, x_ref, sems.at[2]),
-        pltpu.make_async_copy(map_hbm.at[:, 0:128], map_ref, sems.at[3]),
-        pltpu.make_async_copy(parent_hbm.at[:, :, 0:128], west_ref, sems.at[4]),
-        pltpu.make_async_copy(parent_hbm.at[:, :, 384:512], east_ref, sems.at[5]),
-        pltpu.make_async_copy(parent_hbm.at[:, 0:8, :], ends_ref.at[0], sems.at[6]),
-        pltpu.make_async_copy(parent_hbm.at[:, 24:32, :], ends_ref.at[1], sems.at[7]),
+        pltpu.make_async_copy(parent_hbm.at[:, :, 0:128], west_ref, sems.at[0]),
+        pltpu.make_async_copy(parent_hbm.at[:, :, 384:512], east_ref, sems.at[1]),
+        pltpu.make_async_copy(parent_hbm.at[:, 0:8, :], ends_ref.at[0], sems.at[2]),
+        pltpu.make_async_copy(parent_hbm.at[:, 24:32, :], ends_ref.at[1], sems.at[3]),
+        pltpu.make_async_copy(live_hbm, live_ref, sems.at[4]),
+        pltpu.make_async_copy(map_hbm.at[:, 0:128], map_ref, sems.at[5]),
+        pltpu.make_async_copy(w_hbm, w_ref, sems.at[6]),
+        pltpu.make_async_copy(x_hbm, x_ref, sems.at[7]),
     ]
     for copy in copies:
         copy.start()
+    for copy in copies[0:4]:
+        copy.wait()
+    first = lane_rows(ends_ref[0, :, 0, :])
+    last = lane_rows(ends_ref[1, :, 7, :])
+    west = west_ref[...].reshape(128, 128).T[0:1]
+    east = east_ref[...].reshape(128, 128).T[127:128]
+    line = jnp.where(t == 0, first, last)
+    packet_ref[...] = jnp.concatenate([west, east, jnp.zeros((6, 128), jnp.float32), line], 0)
+    sends = [pltpu.make_async_copy(packet_ref, slot_hbm.at[k], sems.at[8 + k]) for k in range(12)]
+    for send in sends:
+        send.start()
+    kept_ref[...] = jnp.where(c == 0, last, first)
+    edge = jnp.where(c == 0, first, last)
+    for copy in copies[4:6]:
+        copy.wait()
+    lane = iota((1, 128), 1)
+    meta = jnp.zeros((1, 128), jnp.int32)
+    for blk in range(4):
+        corner = jnp.where(live_ref[0, blk] != 0, map_ref[blk : blk + 1, 0:1], FAR)
+        meta = jnp.where(lane == META + blk, corner, meta)
     row = iota((48, 96), 0)
     col = iota((48, 96), 1)
     odd = (row >= WROWS).astype(jnp.int32)
@@ -83,7 +106,7 @@
     row = iota((640, 128), 0)
     col = iota((640, 128), 1)
     gather = picks_of((row >> 7) * WIN + (((row & 63) * 43) >> 7) == col)
-    for copy in copies[0:3]:
+    for copy in copies[6:8]:
         copy.wait()
     pieces = []
     for blk in range(4):
@@ -94,34 +117,16 @@
         pieces.append(weight)
     parts = jnp.concatenate(three(jnp.concatenate(pieces, 1)), 0)
     halves = dot(take, parts)
-    lane = iota((WROWS, halves.shape[1]), 1)
-    pooled = jnp.where((lane & 64) == 0, halves[:WROWS], halves[WROWS:])
+    wide = iota((WROWS, halves.shape[1]), 1)
+    pooled = jnp.where((wide & 64) == 0, halves[:WROWS], halves[WROWS:])
     pooled = jnp.concatenate([pooled[:, 640 * b : 640 * (b + 1)] for b in range(4)], 0)
     out_ref[0:OWN] = dot_exact(pooled, gather)
-    for copy in copies[3:8]:
-        copy.wait()
-    lane = iota((1, 128), 1)
-    meta = jnp.zeros((1, 128), jnp.int32)
-    for blk in range(4):
-        corner = jnp.where(live_ref[0, blk] != 0, map_ref[blk : blk + 1, 0:1], FAR)
-        meta = jnp.where(lane == META + blk, corner, meta)
     out_ref[0:1] = jnp.where(lane < META, out_ref[0:1], meta.astype(jnp.float32))
-    first = lane_rows(ends_ref[0, :, 0, :])
-    last = lane_rows(ends_ref[1, :, 7, :])
-    edge = jnp.where(c == 0, first, last)
     for b in range(4):
         out_ref[WROWS * b + WIN : WROWS * (b + 1)] = edge[2 * b : 2 * b + 2]
     out_ref[OWN:ZALL] = edge[8:16]
-    west = west_ref[...].reshape(128, 128).T[0:1]
-    east = east_ref[...].reshape(128, 128).T[127:128]
-    line = jnp.where(t == 0, first, last)
-    packet_ref[0:24] = jnp.concatenate([west, east, jnp.zeros((6, 128), jnp.float32), line], 0)
-    packet_ref[24:40] = jnp.where(c == 0, last, first)
-
-
-def border_kernel(packet_ref, slot_ref):
-    for k in range(12):
-        slot_ref[k] = packet_ref[0:24]
+    for send in sends:
+        send.wait()
 
 
 def inner_kernel(parent_ref, courant_ref, after_ref, out_ref):
@@ -139,29 +144,26 @@
         out_ref[m] = here - u * (here - west) - v * (here - up) + mix * (west + east + up + down - 4.0 * here)
 
 
-def pack_kernel(own_ref, other_ref, slots_ref, links_ref, packet_ref, after_ref, out_ref):
+def lines_kernel(slots_ref, links_ref, side_ref, ends_ref):
     _, x, z, c = place_of()
     panel = lax.axis_index("panel")
-    for s in range(4):
-        out_ref[s, 0:OWN] = own_ref[0:OWN]
-        out_ref[s, OWN:BOTH] = other_ref[0:OWN]
-    passed = jnp.concatenate(
-        [other_ref[WROWS * b + WIN : WROWS * (b + 1)] for b in range(4)] + [other_ref[OWN:ZALL]], 0
-    )
-
     sides = (0, 1, 2 + z)
     links = [(links_ref[panel, s, 0], links_ref[panel, s, 1], links_ref[panel, s, 2]) for s in sides]
+
+    def slot_of(q, half):
+        return lax.rem(6 * half + q + 12 - LEAD, 12)
+
     halves = [(0, z ^ links[0][2]), (1, z ^ links[1][2]), (2, 0), (2, 1)]
     columns = []
     for k, half in halves:
         q, r, _ = links[k]
-        columns.append(slots_ref[2 * q + half, pl.ds(r & 1, 1), :])
+        columns.append(slots_ref[slot_of(q, half), pl.ds(r & 1, 1), :])
     columns = jnp.concatenate(columns + [jnp.zeros((4, 128), jnp.float32)], 0)
     near = iota((128, 128), 0)
     far = iota((128, 128), 1)
     back = dot_exact(columns, picks_of((near ^ 31) == far))
     columns = [jnp.where(links[k][2] == 1, back[i : i + 1], columns[i : i + 1]) for i, (k, _) in enumerate(halves)]
-    lines = jnp.concatenate([slots_ref[2 * q + (r & 1), 8:24, :] for q, r, _ in links], 0)
+    lines = jnp.concatenate([slots_ref[slot_of(q, r & 1), 8:24, :] for q, r, _ in links], 0)
     back = dot_exact(lines, picks_of((near ^ 127) == far))
     lines = [
         jnp.where(
@@ -192,8 +194,8 @@
             for s in range(4):
                 from_column = jnp.where((to_chip == s) & (to_core == core), columns[k], 0.0)
                 from_line = jnp.where(holds[k], cut[4 * s : 4 * s + 1], 0.0)
-                at = SIDES + 2 * k + core
-                out_ref[s, at : at + 1] = jnp.where(r < 2, from_column, from_line)
+                at = 2 * k + core
+                side_ref[s, at : at + 1] = jnp.where(r < 2, from_column, from_line)
 
     q, r, f = links[2]
     to_chip = jnp.where(f == 1, 3 - x, x)
@@ -203,16 +205,28 @@
         piece = jnp.broadcast_to(columns[2 + half], (16, 128))
         piece = spread(jnp.where((lane >> 5) == trc, piece, 0.0))
         ends = jnp.where(((lane >> 5) == group) & (part == to_chip), piece, ends)
-    ends = jnp.where(r < 2, ends, jnp.where(holds[2], lines[2], 0.0))
+    ends_ref[...] = jnp.where(r < 2, ends, jnp.where(holds[2], lines[2], 0.0))
+
+
+def pack_kernel(own_ref, other_ref, kept_ref, side_ref, ends_ref, after_ref, out_ref):
+    _, x, z, c = place_of()
+    passed = jnp.concatenate(
+        [other_ref[WROWS * b + WIN : WROWS * (b + 1)] for b in range(4)] + [other_ref[OWN:ZALL]], 0
+    )
     end_chip = 3 * z
     next_chip = jnp.where(z == 0, x + 1, x - 1)
-    for s in range(4):
+    for j in range(4):
+        s = (XLEAD + j) % 4
+        out_ref[j, 0:OWN] = own_ref[0:OWN]
+        out_ref[j, OWN:BOTH] = other_ref[0:OWN]
+        out_ref[j, SIDES:KEPT] = side_ref[s]
         rows = jnp.where((next_chip == s) & (c != z), passed, 0.0)
-        rows = jnp.where(end_chip == s, ends, rows)
-        for j in range(8):
-            out_ref[s, WROWS * j + WIN : WROWS * (j + 1)] = rows[2 * j : 2 * j + 2]
-    out_ref[x, PASSED:SLOT] = passed
-    out_ref[x, KEPT:PASSED] = packet_ref[24:40]
+        rows = jnp.where(end_chip == s, ends_ref[...], rows)
+        for w in range(8):
+            out_ref[j, WROWS * w + WIN : WROWS * (w + 1)] = rows[2 * w : 2 * w + 2]
+    here = lax.rem(x + 4 - XLEAD, 4)
+    out_ref[here, KEPT:PASSED] = kept_ref[...]
+    out_ref[here, PASSED:SLOT] = passed
 
 
 def deposit(slot_ref, total_ref, meta_ref, corner_ref, list_ref, sem):
@@ -289,8 +303,9 @@
     _, x, z, c = place_of()
     halo = halo_ref[...] + halo_sum(slot_ref)
     ends = halo[8:24]
-    kept = slot_ref[x, KEPT:PASSED]
-    passed = slot_ref[x, PASSED:SLOT]
+    chip = lax.rem(x + 4 - XLEAD, 4)
+    kept = slot_ref[chip, KEPT:PASSED]
+    passed = slot_ref[chip, PASSED:SLOT]
     north = jnp.where(c == 1, kept, jnp.where(z == 0, ends, passed))
     south = jnp.where(c == 0, kept, jnp.where(z == 0, passed, ends))
     west = jnp.where(c == 0, halo[0:1], halo[1:2])
@@ -336,11 +351,11 @@
     courant = courant[0, 0]
     values = nest_tracer[0, :, 0].reshape(4, 4, 32, 128).transpose(0, 2, 1, 3).reshape(4, 128, 128)
     weights = nest_weight[0].reshape(4, 32, 128).transpose(1, 0, 2).reshape(128, 128)
-    own, packet = pl.pallas_call(
+    own, slots, kept = pl.pallas_call(
         pool_kernel,
-        out_shape=(shape(ZALL, 128), shape(40, 128)),
+        out_shape=(shape(ZALL, 128), shape(12, 24, 128), shape(16, 128)),
         in_specs=[ANY] * 5,
-        out_specs=(VMEM, VMEM),
+        out_specs=(VMEM, ANY, VMEM),
         scratch_shapes=[
             pltpu.VMEM((4, 128, 128), jnp.float32),
             pltpu.VMEM((128, 128), jnp.float32),
@@ -349,38 +364,40 @@
             pltpu.VMEM((4, 32, 128), jnp.float32),
             pltpu.VMEM((4, 32, 128), jnp.float32),
             pltpu.VMEM((2, 4, 8, 512), jnp.float32),
-            dma(8),
+            pltpu.VMEM((24, 128), jnp.float32),
+            dma(20),
         ],
         compiler_params=params,
     )(*[pltpu.with_memory_space_constraint(a, pltpu.HBM) for a in (values, weights, nest_map[0], parent, block_live)])
     other = lax.ppermute(own, "tile", [(t, t ^ 2) for t in range(16)])
-    slots = pl.pallas_call(
-        border_kernel,
-        out_shape=shape(12, 24, 128),
-        in_specs=[VMEM],
-        out_specs=VMEM,
-        compiler_params=params,
-    )(packet)
+    around = [(LEAD + j) % 12 for j in range(12)]
     lines_of_z = [
-        [p * 16 + tile_of(x, z, c) for p in range(6) for z in range(2)] for x in range(4) for c in range(2)
+        [(zz % 6) * 16 + tile_of(x, zz // 6, c) for zz in around] for x in range(4) for c in range(2)
     ]
     slots = lax.all_to_all(slots, ("panel", "tile"), 0, 0, tiled=True, axis_index_groups=lines_of_z)
+    side, ends = pl.pallas_call(
+        lines_kernel,
+        out_shape=(shape(4, 8, 128), shape(16, 128)),
+        in_specs=[VMEM, SMEM],
+        out_specs=(VMEM, VMEM),
+        compiler_params=params,
+    )(slots, edge_links)
     inner = pl.pallas_call(
         inner_kernel,
         out_shape=shape(4, 32, 512),
         in_specs=[VMEM, VMEM, ANY],
         out_specs=VMEM,
         compiler_params=params,
-        cost_estimate=cost(1 << 24),
-    )(parent, courant, other)
+        cost_estimate=cost(1 << 20),
+    )(parent, courant, own)
     packed = pl.pallas_call(
         pack_kernel,
         out_shape=shape(4, SLOT, 128),
-        in_specs=[VMEM, VMEM, VMEM, SMEM, VMEM, ANY],
+        in_specs=[VMEM, VMEM, VMEM, VMEM, VMEM, ANY],
         out_specs=VMEM,
         compiler_params=params,
-    )(own, other, slots, edge_links, packet, inner)
-    chips = [[tile_of(x, z, c) for x in range(4)] for z in range(2) for c in range(2)]
+    )(own, other, kept, side, ends, inner)
+    chips = [[tile_of((XLEAD + j) % 4, z, c) for j in range(4)] for z in range(2) for c in range(2)]
     near = lax.all_to_all(packed, "tile", 0, 0, tiled=True, axis_index_groups=chips)
     far = lax.ppermute(near, "tile", [(t, t ^ 1) for t in range(16)])
     scratch = [

time: 53.3 us -> 48.3 us (0.906)
  waiting for transfers between devices: 5.14 us -> 3.4 us
  blocking collectives: 10.8 us -> 9.11 us
  starting transfers between devices: 30.3 us -> 29.1 us
    ppermute x1, starting transfers between devices: 9.63 us -> 7.03 us  [body(): other = lax.ppermute(own, 'tile', [(t, t ^ 2) for t in range(16)])]
    ppermute x1, waiting for transfers between devices: 4.88 us -> 3.13 us  [body(): other = lax.ppermute(own, 'tile', [(t, t ^ 2) for t in range(16)])]
    all_to_all x1, blocking collectives: 10.8 us -> 9.11 us  [body(): lax.all_to_all(packed, 'tile', 0, 0, tiled=True, axis_index_groups=chips)]
    pallas_call x1, Pallas kernels: 1.03 us -> 0.04 us  [body(): pl.pallas_call(pack_kernel, out_shape=shape(4, SLOT, 128), in_specs=[VMEM...]
    all_to_all x1, starting transfers between devices: 15.8 us -> 16.7 us  [body(): lax.all_to_all(slots, ('panel', 'tile'), 0, 0, tiled=True, axis_index_gro...]
    pallas_call x2, Pallas kernels: 2.33 us -> 2.93 us  [the longest x1 1.89 us: body(): pl.pallas_call(pool_kernel, out_shape=(shape(ZALL, 128), shape(12, 24, 12...]
  transfers between devices with their start and end apart: 3 -> 3, of which waited for: 2 -> 2; matrix products, arithmetic and copies ran while one was open for 0% -> 0% of each run, Pallas kernels for 3% -> 5%
where the time goes in v3:
time: 48.3 us; the launch traced here: 48 us
  starting transfers between devices  29.1 us (60%)
  blocking collectives  9.11 us (19%)
  Pallas kernels  6.18 us (13%)
  waiting for transfers between devices  3.4 us (7%)
    all_to_all x1, starting transfers between devices, body(): lax.all_to_all(slots, ('panel', 'tile'), 0, 0, tiled=True, axis_index_gro...  16.7 us
    all_to_all x1, blocking collectives, body(): lax.all_to_all(packed, 'tile', 0, 0, tiled=True, axis_index_groups=chips)  9.11 us
    ppermute x1, starting transfers between devices, body(): other = lax.ppermute(own, 'tile', [(t, t ^ 2) for t in range(16)])  7.03 us
    ppermute x1, starting transfers between devices, body(): far = lax.ppermute(near, 'tile', [(t, t ^ 1) for t in range(16)])  5.31 us
    ppermute x1, waiting for transfers between devices, body(): other = lax.ppermute(own, 'tile', [(t, t ^ 2) for t in range(16)])  3.13 us
    pallas_call x1, Pallas kernels, body(): pl.pallas_call(pool_kernel, out_shape=(shape(ZALL, 128), shape(12, 24, 12...  1.89 us
    pallas_call x1, Pallas kernels, body(): pl.pallas_call(final_kernel, out_shape=shape(4, 32, 512), in_specs=[VMEM,...  1.81 us
    pallas_call x1, Pallas kernels, body(): pl.pallas_call(near_kernel, out_shape=(shape(5, 32, 512), shape(24, 128))...  1.17 us
  transfers between devices with their start and end apart: 3, of which 2 were waited for; matrix products, arithmetic and copies ran while one was open for 0% of the time, Pallas kernels for 5%

profile of v3, /device:TPU:1, one launch (start us, length us, event | category | flops | bytes accessed | tf_op | source)
XLA Modules:
  0.0 48.0 jit_solution(5423546251223647065)
XLA Ops:
  0.0 0.0 copy-start.1
  0.0 1.9 %shard_map.73 = (f32[104,128]{1,0:T(8,128)S(1)}, f32[12,24,128]{2,1,0:T(8,128)}, f32[16,128]{1,0:T(8,128)S(1)}) custom-call(f32[4,128,128]{2,1,0:T(8,128)} %bitcast.18, f32[128,128]{1,0:T(8,128)} %bitcast.19, s32[4,4096]{1,0:T(4,128)} %bitcast.20, f32[4,32,512]{2,1,0:T(8,128)} %bitcast.14, s32[1,4]{1,0:T(1,128)} %live_hbm.1), custom_call_target="tpu_custom_call" | custom-call | tf_op jit(solution)/shard_map/pallas_call | solution.py:354
  1.9 0.0 copy-start
  1.9 0.0 copy-start.2
  1.9 16.7 %all-to-all-start = ((f32[12,24,128]{2,1,0:T(8,128)}), f32[12,24,128]{2,1,0:T(8,128)S(1)}, u32[]{:S(2)}, u32[]{:S(2)}) async-start(f32[12,24,128]{2,1,0:T(8,128)} %get-tuple-element.14), calls=%async_computation | async-start | bytes 294912 | tf_op jit(solution)/shard_map/all_to_all | solution.py:377
  18.7 7.0 %collective-permute-start = (f32[104,128]{1,0:T(8,128)S(1)}, f32[104,128]{1,0:T(8,128)S(1)}, u32[]{:S(2)}, u32[]{:S(2)}) collective-permute-start(f32[104,128]{1,0:T(8,128)S(1)} %get-tuple-element.12.after_ref.own_ref), channel_id=1, source_target_pairs={{0,16},{8,24},{16,0},{24,8},{32,48},{40,56},{48,32},{56,40},{64,80... | collective-permute-start | bytes 159752 | tf_op jit(solution)/shard_map/ppermute | solution.py:372
  25.7 0.0 copy-done.2
  25.7 0.1 copy.10.links_ref
  25.8 0.0 copy-done.1
  25.8 0.0 copy-done
  25.8 0.2 shard_map.75.after_ref.inner_ref
  26.1 0.0 all-to-all-done.slots_ref
  26.1 1.0 %shard_map.74 = (f32[4,8,128]{2,1,0:T(8,128)S(1)}, f32[16,128]{1,0:T(8,128)S(1)}) custom-call(f32[12,24,128]{2,1,0:T(8,128)S(1)} %all-to-all-done.slots_ref, s32[6,4,3]{2,1,0:T(4,128)S(1)} %copy.10.links_ref), custom_call_target="tpu_custom_call" | custom-call | tf_op jit(solution)/shard_map/pallas_call | solution.py:378
  27.1 3.1 %collective-permute-done.other_ref = f32[104,128]{1,0:T(8,128)S(1)} collective-permute-done((f32[104,128]{1,0:T(8,128)S(1)}, f32[104,128]{1,0:T(8,128)S(1)}, u32[]{:S(2)}, u32[]{:S(2)}) %collective-permute-start) | collective-permute-done | bytes 53280 | tf_op jit(solution)/shard_map/ppermute | solution.py:372
  30.3 9.1 %all_to_all.10.slot_ref = f32[4,232,128]{2,1,0:T(8,128)S(1)} all-to-all(f32[4,232,128]{2,1,0:T(8,128)S(1)} %shard_map.76), channel_id=1, replica_groups={{64,96,0,32},{72,104,8,40},{80,112,16,48},{88,120,24,56},{65,97,1,33},{..., dimensions={0} | all-to-all | bytes 950272 | tf_op jit(solution)/shard_map/all_to_all | solution.py:401
  39.4 5.3 %collective-permute-start.1 = (f32[4,232,128]{2,1,0:T(8,128)S(1)}, f32[4,232,128]{2,1,0:T(8,128)S(1)}, u32[]{:S(2)}, u32[]{:S(2)}) collective-permute-start(f32[4,232,128]{2,1,0:T(8,128)S(1)} %all_to_all.10.slot_ref), channel_id=1, source_target_pairs={{0,8},{8,0},{16,24},{24,16},{32,40},{40,32},{48,56},{56,48},{64,72... | collective-permute-start | bytes 1425416 | tf_op jit(solution)/shard_map/ppermute | solution.py:402
  44.7 1.2 %shard_map.77 = (f32[5,32,512]{2,1,0:T(8,128)S(1)}, f32[24,128]{1,0:T(8,128)S(1)}) custom-call(f32[4,232,128]{2,1,0:T(8,128)S(1)} %all_to_all.10.slot_ref, f32[4,32,512]{2,1,0:T(8,128)S(1)} %shard_map.75.after_ref.inner_ref), custom_call_target="tpu_custom_call" | custom-call | flops 1048576 | bytes 1048576 | tf_op jit(solution)/shard_map/pallas_call | solution.py:410
  45.9 0.3 collective-permute-done.1.slot_ref
  46.2 1.8 %shard_map.78 = f32[4,32,512]{2,1,0:T(8,128)} custom-call(f32[4,232,128]{2,1,0:T(8,128)S(1)} %collective-permute-done.1.slot_ref, f32[5,32,512]{2,1,0:T(8,128)S(1)} %get-tuple-element.17.near_ref, f32[24,128]{1,0:T(8,128)S(1)} %get-tuple-element.18.halo_ref, f32[3,32,512]{2,1,0:T(8,128)S(1)} %bitcast.17), custom_call_target="tpu_custom_call" | custom-call | tf_op jit(solution)/shard_map/pallas_call | solution.py:419
  (1 shorter events, 0.0 us)
Async XLA Ops:
  0.0 25.8 %copy-start.1 = (f32[1,1,3,32,512]{4,3,2,1,0:T(8,128)S(1)}, f32[1,1,3,32,512]{4,3,2,1,0:T(8,128)}, u32[]{:S(2)}) copy-start(f32[1,1,3,32,512]{4,3,2,1,0:T(8,128)} %param.8) | copy-start | bytes 589828
  1.9 23.9 %copy-start = (f32[1,1,4,32,512]{4,3,2,1,0:T(8,128)S(1)}, f32[1,1,4,32,512]{4,3,2,1,0:T(8,128)}, u32[]{:S(2)}) copy-start(f32[1,1,4,32,512]{4,3,2,1,0:T(8,128)} %param.7) | copy-start | bytes 786436
  1.9 23.8 %copy-start.2 = (s32[6,4,3]{0,1,2:T(4,128)S(1)}, s32[6,4,3]{0,1,2:T(4,128)}, u32[]{:S(2)}) copy-start(s32[6,4,3]{0,1,2:T(4,128)} %param.9) | copy-start | bytes 868
  1.9 24.1 %all-to-all-start = ((f32[12,24,128]{2,1,0:T(8,128)}), f32[12,24,128]{2,1,0:T(8,128)S(1)}, u32[]{:S(2)}, u32[]{:S(2)}) async-start(f32[12,24,128]{2,1,0:T(8,128)} %get-tuple-element.14), calls=%async_computation | async-start | bytes 294912 | tf_op jit(solution)/shard_map/all_to_all | solution.py:377
  18.7 11.6 %collective-permute-start = (f32[104,128]{1,0:T(8,128)S(1)}, f32[104,128]{1,0:T(8,128)S(1)}, u32[]{:S(2)}, u32[]{:S(2)}) collective-permute-start(f32[104,128]{1,0:T(8,128)S(1)} %get-tuple-element.12.after_ref.own_ref), channel_id=1, source_target_pairs={{0,16},{8,24},{16,0},{24,8},{32,48},{40,56},{48,32},{56,40},{64,80... | collective-permute-start | bytes 159752 | tf_op jit(solution)/shard_map/ppermute | solution.py:372
  39.4 6.8 %collective-permute-start.1 = (f32[4,232,128]{2,1,0:T(8,128)S(1)}, f32[4,232,128]{2,1,0:T(8,128)S(1)}, u32[]{:S(2)}, u32[]{:S(2)}) collective-permute-start(f32[4,232,128]{2,1,0:T(8,128)S(1)} %all_to_all.10.slot_ref), channel_id=1, source_target_pairs={{0,8},{8,0},{16,24},{24,16},{32,40},{40,32},{48,56},{56,48},{64,72... | collective-permute-start | bytes 1425416 | tf_op jit(solution)/shard_map/ppermute | solution.py:402

commit v4 on v3

--- a/solution.py
+++ b/solution.py
@@ -9,13 +9,9 @@
 WROWS = 24
 FAR = -(64 * 512)
 OWN = 4 * WROWS
-ZALL = OWN + 8
-BOTH = 2 * OWN
-SIDES = BOTH
-KEPT = SIDES + 8
-PASSED = KEPT + 16
-SLOT = PASSED + 16
-META = 112
+SLOT = 2 * OWN
+META = 110
+FREE = 112
 LEAD = 10
 XLEAD = 2
 VMEM = pl.BlockSpec(memory_space=pltpu.VMEM)
@@ -61,43 +57,49 @@
     return lax.broadcasted_iota(jnp.int32, dims, axis)
 
 
+def to_free(rows, g):
+    return pltpu.roll(rows, (FREE - 16 * g) % 128, 1)
+
+
+def from_free(parts):
+    lane = iota(parts[0].shape, 1) >> 4
+    rows = jnp.zeros_like(parts[0])
+    for g in range(8):
+        rows = jnp.where(lane == g, pltpu.roll(parts[g], (16 * g - FREE + 128) % 128, 1), rows)
+    return rows
+
+
 def pool_kernel(
     x_hbm, w_hbm, map_hbm, parent_hbm, live_hbm, out_ref, slot_hbm, kept_ref,
-    x_ref, w_ref, map_ref, live_ref, west_ref, east_ref, ends_ref, packet_ref, sems
+    x_ref, w_ref, map_ref, live_ref, parent_ref, packet_ref, sems
 ):
     t, _, _, c = place_of()
     copies = [
-        pltpu.make_async_copy(parent_hbm.at[:, :, 0:128], west_ref, sems.at[0]),
-        pltpu.make_async_copy(parent_hbm.at[:, :, 384:512], east_ref, sems.at[1]),
-        pltpu.make_async_copy(parent_hbm.at[:, 0:8, :], ends_ref.at[0], sems.at[2]),
-        pltpu.make_async_copy(parent_hbm.at[:, 24:32, :], ends_ref.at[1], sems.at[3]),
-        pltpu.make_async_copy(live_hbm, live_ref, sems.at[4]),
-        pltpu.make_async_copy(map_hbm.at[:, 0:128], map_ref, sems.at[5]),
-        pltpu.make_async_copy(w_hbm, w_ref, sems.at[6]),
-        pltpu.make_async_copy(x_hbm, x_ref, sems.at[7]),
+        pltpu.make_async_copy(parent_hbm, parent_ref, sems.at[0]),
+        pltpu.make_async_copy(live_hbm, live_ref, sems.at[1]),
+        pltpu.make_async_copy(map_hbm.at[:, 0:128], map_ref, sems.at[2]),
+        pltpu.make_async_copy(w_hbm, w_ref, sems.at[3]),
+        pltpu.make_async_copy(x_hbm, x_ref, sems.at[4]),
     ]
     for copy in copies:
         copy.start()
-    for copy in copies[0:4]:
-        copy.wait()
-    first = lane_rows(ends_ref[0, :, 0, :])
-    last = lane_rows(ends_ref[1, :, 7, :])
-    west = west_ref[...].reshape(128, 128).T[0:1]
-    east = east_ref[...].reshape(128, 128).T[127:128]
+    copies[0].wait()
+    first = parent_ref[:, 0, :]
+    last = parent_ref[:, 31, :]
+    west = parent_ref[:, :, 0:128].reshape(128, 128).T[0:1]
+    east = parent_ref[:, :, 384:512].reshape(128, 128).T[127:128]
     line = jnp.where(t == 0, first, last)
-    packet_ref[...] = jnp.concatenate([west, east, jnp.zeros((6, 128), jnp.float32), line], 0)
-    sends = [pltpu.make_async_copy(packet_ref, slot_hbm.at[k], sems.at[8 + k]) for k in range(12)]
-    for send in sends:
-        send.start()
+    packet = jnp.concatenate([west, east, jnp.zeros((6, 128), jnp.float32), lane_rows(line)], 0)
+    for k in range(12):
+        packet_ref[k] = packet
+    send = pltpu.make_async_copy(packet_ref, slot_hbm, sems.at[5])
+    send.start()
+    first = lane_rows(first)
+    last = lane_rows(last)
     kept_ref[...] = jnp.where(c == 0, last, first)
     edge = jnp.where(c == 0, first, last)
-    for copy in copies[4:6]:
+    for copy in copies[1:3]:
         copy.wait()
-    lane = iota((1, 128), 1)
-    meta = jnp.zeros((1, 128), jnp.int32)
-    for blk in range(4):
-        corner = jnp.where(live_ref[0, blk] != 0, map_ref[blk : blk + 1, 0:1], FAR)
-        meta = jnp.where(lane == META + blk, corner, meta)
     row = iota((48, 96), 0)
     col = iota((48, 96), 1)
     odd = (row >= WROWS).astype(jnp.int32)
@@ -106,7 +108,7 @@
     row = iota((640, 128), 0)
     col = iota((640, 128), 1)
     gather = picks_of((row >> 7) * WIN + (((row & 63) * 43) >> 7) == col)
-    for copy in copies[6:8]:
+    for copy in copies[3:5]:
         copy.wait()
     pieces = []
     for blk in range(4):
@@ -120,13 +122,22 @@
     wide = iota((WROWS, halves.shape[1]), 1)
     pooled = jnp.where((wide & 64) == 0, halves[:WROWS], halves[WROWS:])
     pooled = jnp.concatenate([pooled[:, 640 * b : 640 * (b + 1)] for b in range(4)], 0)
-    out_ref[0:OWN] = dot_exact(pooled, gather)
-    out_ref[0:1] = jnp.where(lane < META, out_ref[0:1], meta.astype(jnp.float32))
+    windows = dot_exact(pooled, gather)
+    rest = jnp.zeros((8, 128), jnp.float32)
+    extra = [e for b in range(4) for e in (to_free(edge[8:16], 2 * b), to_free(edge[8:16], 2 * b + 1), rest)]
+    lane = iota((OWN, 128), 1)
+    out_ref[...] = jnp.where(lane < FREE, windows, jnp.concatenate(extra, 0))
+    lane = iota((1, 128), 1)
+    for k in range(2):
+        row = out_ref[k : k + 1]
+        for e in range(2):
+            blk = 2 * k + e
+            corner = jnp.where(live_ref[0, blk] != 0, map_ref[blk : blk + 1, 0:1], FAR)
+            row = jnp.where(lane == META + e, corner.astype(jnp.float32), row)
+        out_ref[k : k + 1] = row
     for b in range(4):
         out_ref[WROWS * b + WIN : WROWS * (b + 1)] = edge[2 * b : 2 * b + 2]
-    out_ref[OWN:ZALL] = edge[8:16]
-    for send in sends:
-        send.wait()
+    send.wait()
 
 
 def inner_kernel(parent_ref, courant_ref, after_ref, out_ref):
@@ -210,39 +221,58 @@
 
 def pack_kernel(own_ref, other_ref, kept_ref, side_ref, ends_ref, after_ref, out_ref):
     _, x, z, c = place_of()
-    passed = jnp.concatenate(
-        [other_ref[WROWS * b + WIN : WROWS * (b + 1)] for b in range(4)] + [other_ref[OWN:ZALL]], 0
-    )
+    passed = from_free([other_ref[WROWS * (g // 2) + 8 * (g % 2) : WROWS * (g // 2) + 8 * (g % 2) + 8] for g in range(8)])
+    passed = jnp.concatenate([other_ref[WROWS * b + WIN : WROWS * (b + 1)] for b in range(4)] + [passed], 0)
+    kept = kept_ref[...]
+    ends = ends_ref[...]
+    high = iota((16, 128), 1) < FREE
+    low = iota((8, 128), 1) < FREE
     end_chip = 3 * z
     next_chip = jnp.where(z == 0, x + 1, x - 1)
     for j in range(4):
         s = (XLEAD + j) % 4
-        out_ref[j, 0:OWN] = own_ref[0:OWN]
-        out_ref[j, OWN:BOTH] = other_ref[0:OWN]
-        out_ref[j, SIDES:KEPT] = side_ref[s]
+        side = side_ref[s]
         rows = jnp.where((next_chip == s) & (c != z), passed, 0.0)
-        rows = jnp.where(end_chip == s, ends_ref[...], rows)
+        rows = jnp.where(end_chip == s, ends, rows)
+        rows = jnp.where((x == s) & (c == z), passed, rows)
         for w in range(8):
-            out_ref[j, WROWS * w + WIN : WROWS * (w + 1)] = rows[2 * w : 2 * w + 2]
-    here = lax.rem(x + 4 - XLEAD, 4)
-    out_ref[here, KEPT:PASSED] = kept_ref[...]
-    out_ref[here, PASSED:SLOT] = passed
-
-
-def deposit(slot_ref, total_ref, meta_ref, corner_ref, list_ref, sem):
-    t = lax.axis_index("tile")
-    first_row = 32 * t
-    meta = jnp.concatenate([slot_ref[i // 2, OWN * (i % 2) : OWN * (i % 2) + 1, :] for i in range(8)], 0)
+            window_ref = own_ref if w < 4 else other_ref
+            at = WROWS * (w % 4)
+            to = WROWS * w
+            out_ref[j, to : to + 16] = jnp.where(high, window_ref[at : at + 16], to_free(kept, w))
+            out_ref[j, to + 16 : to + 24] = jnp.where(low, window_ref[at + 16 : at + 24], to_free(side, w))
+            out_ref[j, to + WIN : to + WROWS] = rows[2 * w : 2 * w + 2]
+
+
+def halo_sum(slot_ref, skip):
+    sides = []
+    for w in range(8):
+        at = WROWS * w + 16
+        sides.append(slot_ref[0, at : at + 8] + slot_ref[1, at : at + 8] + slot_ref[2, at : at + 8] + slot_ref[3, at : at + 8])
+    ends = jnp.zeros((16, 128), jnp.float32)
+    for s in range(4):
+        rows = jnp.concatenate([slot_ref[s, WROWS * w + WIN : WROWS * (w + 1), :] for w in range(8)], 0)
+        ends = ends + jnp.where(skip == s, 0.0, rows)
+    return jnp.concatenate([from_free(sides), ends], 0)
+
+
+def deposit_start(slot_ref, total_ref, meta_ref, corner_ref, sem):
+    first_row = 32 * lax.axis_index("tile")
+    meta = jnp.concatenate([slot_ref[i // 2, OWN * (i % 2) : OWN * (i % 2) + 2, :] for i in range(8)], 0)
     meta = meta.astype(jnp.int32)
     r = (meta >> 9) - first_row
     meta_ref[...] = jnp.where((r > -(WIN + 1)) & (r < 32), meta, -1)
     copy = pltpu.make_async_copy(meta_ref, corner_ref, sem)
     copy.start()
     total_ref[:, 16:56, :] = jnp.zeros((5, 40, 640), jnp.float32)
-    copy.wait()
+    return copy
+
+
+def deposit(slot_ref, total_ref, corner_ref, list_ref):
+    first_row = 32 * lax.axis_index("tile")
     count = jnp.int32(0)
     for i in range(32):
-        corner = corner_ref[i // 4, META + i % 4]
+        corner = corner_ref[i // 2, META + i % 2]
         list_ref[0, count] = corner
         list_ref[1, count] = i
         count = count + jnp.where(corner >= 0, 1, 0)
@@ -281,56 +311,54 @@
     return jnp.concatenate([mass[:, 0:128] + spill, mass[:, 128:512]], 1)
 
 
-def halo_sum(slot_ref):
-    total = slot_ref[0, SIDES:KEPT]
-    ends = None
-    for s in range(4):
-        rows = jnp.concatenate([slot_ref[s, WROWS * j + WIN : WROWS * (j + 1), :] for j in range(8)], 0)
-        ends = rows if s == 0 else ends + rows
-        total = total if s == 0 else total + slot_ref[s, SIDES:KEPT]
-    return jnp.concatenate([total, ends], 0)
-
-
-def near_kernel(slot_ref, inner_ref, out_ref, halo_ref, total_ref, meta_ref, corner_ref, list_ref, sem):
-    deposit(slot_ref, total_ref, meta_ref, corner_ref, list_ref, sem)
+def near_kernel(slot_ref, inner_ref, end_ref, out_ref, halo_ref, total_ref, meta_ref, corner_ref, list_ref, sem):
+    _, x, z, c = place_of()
+    copy = deposit_start(slot_ref, total_ref, meta_ref, corner_ref, sem)
+    halo = halo_sum(slot_ref, lax.rem(x + 4 - XLEAD, 4))
+    halo_ref[0:8] = halo[0:8]
+    halo_ref[8:24] = halo[8:24] + jnp.where((x == 3 * z) & (c == z), end_ref[...], 0.0)
+    copy.wait()
+    deposit(slot_ref, total_ref, corner_ref, list_ref)
     for m in range(4):
         out_ref[m] = inner_ref[m] + deposited(total_ref, m)
     out_ref[4] = 1.0 + deposited(total_ref, 4)
-    halo_ref[...] = halo_sum(slot_ref)
 
 
 def final_kernel(slot_ref, near_ref, halo_ref, courant_ref, out_ref, total_ref, meta_ref, corner_ref, list_ref, sem):
     _, x, z, c = place_of()
-    halo = halo_ref[...] + halo_sum(slot_ref)
-    ends = halo[8:24]
+    copy = deposit_start(slot_ref, total_ref, meta_ref, corner_ref, sem)
+    halo = halo_ref[...] + halo_sum(slot_ref, -1)
     chip = lax.rem(x + 4 - XLEAD, 4)
-    kept = slot_ref[chip, KEPT:PASSED]
-    passed = slot_ref[chip, PASSED:SLOT]
-    north = jnp.where(c == 1, kept, jnp.where(z == 0, ends, passed))
-    south = jnp.where(c == 0, kept, jnp.where(z == 0, passed, ends))
+    kept = from_free([slot_ref[chip, WROWS * w : WROWS * w + 16, :] for w in range(8)])
+    passed = jnp.concatenate([slot_ref[chip, WROWS * w + WIN : WROWS * (w + 1), :] for w in range(8)], 0)
+    crossing = jnp.where(c == z, halo[8:24], passed)
+    north = jnp.where(c == 0, crossing, kept)
+    south = jnp.where(c == 0, kept, crossing)
     west = jnp.where(c == 0, halo[0:1], halo[1:2])
     east = jnp.where(c == 0, halo[2:3], halo[3:4])
     west = jnp.broadcast_to(west, (128, 128)).T
     east = jnp.broadcast_to(east, (128, 128)).T
-    deposit(slot_ref, total_ref, meta_ref, corner_ref, list_ref, sem)
-    u = courant_ref[0]
     v = courant_ref[1]
     mix = courant_ref[2]
     lane = iota((32, 128), 1)
-    first = jnp.where(lane == 0, u[:, 0:128] + mix[:, 0:128], 0.0)
+    first = jnp.where(lane == 0, courant_ref[0, :, 0:128] + mix[:, 0:128], 0.0)
     last = jnp.where(lane == 127, mix[:, 384:512], 0.0)
     line = iota((32, 512), 0)
     above = jnp.where(line == 0, v + mix, 0.0)
     below = jnp.where(line == 31, mix, 0.0)
-    scale = 1.0 / (near_ref[4] + deposited(total_ref, 4))
     for m in range(4):
-        value = near_ref[m] + deposited(total_ref, m)
+        value = near_ref[m]
         north_row = jnp.concatenate([north[4 * k + m : 4 * k + m + 1] for k in range(4)], 1)
         south_row = jnp.concatenate([south[4 * k + m : 4 * k + m + 1] for k in range(4)], 1)
         value = value + above * north_row + below * south_row
         left = value[:, 0:128] + first * west[32 * m : 32 * m + 32]
         right = value[:, 384:512] + last * east[32 * m : 32 * m + 32]
-        out_ref[m] = jnp.concatenate([left, value[:, 128:384], right], 1) * scale
+        out_ref[m] = jnp.concatenate([left, value[:, 128:384], right], 1)
+    copy.wait()
+    deposit(slot_ref, total_ref, corner_ref, list_ref)
+    scale = 1.0 / (near_ref[4] + deposited(total_ref, 4))
+    for m in range(4):
+        out_ref[m] = (out_ref[m] + deposited(total_ref, m)) * scale
 
 
 def shape(*dims):
@@ -353,7 +381,7 @@
     weights = nest_weight[0].reshape(4, 32, 128).transpose(1, 0, 2).reshape(128, 128)
     own, slots, kept = pl.pallas_call(
         pool_kernel,
-        out_shape=(shape(ZALL, 128), shape(12, 24, 128), shape(16, 128)),
+        out_shape=(shape(OWN, 128), shape(12, 24, 128), shape(16, 128)),
         in_specs=[ANY] * 5,
         out_specs=(VMEM, ANY, VMEM),
         scratch_shapes=[
@@ -361,11 +389,9 @@
             pltpu.VMEM((128, 128), jnp.float32),
             pltpu.VMEM((4, 128), jnp.int32),
             pltpu.SMEM((1, 4), jnp.int32),
-            pltpu.VMEM((4, 32, 128), jnp.float32),
-            pltpu.VMEM((4, 32, 128), jnp.float32),
-            pltpu.VMEM((2, 4, 8, 512), jnp.float32),
-            pltpu.VMEM((24, 128), jnp.float32),
-            dma(20),
+            pltpu.VMEM((4, 32, 512), jnp.float32),
+            pltpu.VMEM((12, 24, 128), jnp.float32),
+            dma(6),
         ],
         compiler_params=params,
     )(*[pltpu.with_memory_space_constraint(a, pltpu.HBM) for a in (values, weights, nest_map[0], parent, block_live)])
@@ -402,20 +428,20 @@
     far = lax.ppermute(near, "tile", [(t, t ^ 1) for t in range(16)])
     scratch = [
         pltpu.VMEM((5, 88, 640), jnp.float32),
-        pltpu.VMEM((8, 128), jnp.int32),
-        pltpu.SMEM((8, 128), jnp.int32),
+        pltpu.VMEM((16, 128), jnp.int32),
+        pltpu.SMEM((16, 128), jnp.int32),
         pltpu.SMEM((2, 40), jnp.int32),
         pltpu.SemaphoreType.DMA,
     ]
     summed, halo = pl.pallas_call(
         near_kernel,
         out_shape=(shape(5, 32, 512), shape(24, 128)),
-        in_specs=[VMEM, VMEM],
+        in_specs=[VMEM, VMEM, VMEM],
         out_specs=(VMEM, VMEM),
         scratch_shapes=scratch,
         compiler_params=params,
         cost_estimate=cost(1 << 20),
-    )(near, inner)
+    )(near, inner, ends)
     out = pl.pallas_call(
         final_kernel,
         out_shape=shape(4, 32, 512),

time: 48.3 us -> 48 us (level)
  no operation moved by 1% of the time
where the time goes in v4:
time: 48 us; the launch traced here: 47.7 us
  starting transfers between devices  29.1 us (61%)
  blocking collectives  8.68 us (18%)
  Pallas kernels  6.48 us (14%)
  waiting for transfers between devices  3.3 us (7%)
    all_to_all x1, starting transfers between devices, body(): lax.all_to_all(slots, ('panel', 'tile'), 0, 0, tiled=True, axis_index_gro...  16.7 us
    all_to_all x1, blocking collectives, body(): lax.all_to_all(packed, 'tile', 0, 0, tiled=True, axis_index_groups=chips)  8.68 us
    ppermute x1, starting transfers between devices, body(): other = lax.ppermute(own, 'tile', [(t, t ^ 2) for t in range(16)])  7.03 us
    ppermute x1, starting transfers between devices, body(): far = lax.ppermute(near, 'tile', [(t, t ^ 1) for t in range(16)])  5.31 us
    ppermute x1, waiting for transfers between devices, body(): other = lax.ppermute(own, 'tile', [(t, t ^ 2) for t in range(16)])  3.09 us
    pallas_call x1, Pallas kernels, body(): pl.pallas_call(final_kernel, out_shape=shape(4, 32, 512), in_specs=[VMEM,...  2.18 us
    pallas_call x1, Pallas kernels, body(): pl.pallas_call(pool_kernel, out_shape=(shape(OWN, 128), shape(12, 24, 128...  1.81 us
    pallas_call x1, Pallas kernels, body(): pl.pallas_call(near_kernel, out_shape=(shape(5, 32, 512), shape(24, 128))...  1.11 us
  transfers between devices with their start and end apart: 3, of which 2 were waited for; matrix products, arithmetic and copies ran while one was open for 0% of the time, Pallas kernels for 5%

profile of v4, /device:TPU:1, one launch (start us, length us, event | category | flops | bytes accessed | tf_op | source)
XLA Modules:
  0.0 47.7 jit_solution(4214838301821292310)
XLA Ops:
  0.0 0.0 copy-start.1
  0.0 1.8 %shard_map.73 = (f32[96,128]{1,0:T(8,128)S(1)}, f32[12,24,128]{2,1,0:T(8,128)}, f32[16,128]{1,0:T(8,128)S(1)}) custom-call(f32[4,128,128]{2,1,0:T(8,128)} %bitcast.18, f32[128,128]{1,0:T(8,128)} %bitcast.19, s32[4,4096]{1,0:T(4,128)} %bitcast.20, f32[4,32,512]{2,1,0:T(8,128)} %bitcast.14, s32[1,4]{1,0:T(1,128)} %live_hbm.1), custom_call_target="tpu_custom_call" | custom-call | tf_op jit(solution)/shard_map/pallas_call | solution.py:382
  1.8 0.0 copy-start
  1.8 0.0 copy-start.2
  1.8 16.7 %all-to-all-start = ((f32[12,24,128]{2,1,0:T(8,128)}), f32[12,24,128]{2,1,0:T(8,128)S(1)}, u32[]{:S(2)}, u32[]{:S(2)}) async-start(f32[12,24,128]{2,1,0:T(8,128)} %get-tuple-element.14), calls=%async_computation | async-start | bytes 294912 | tf_op jit(solution)/shard_map/all_to_all | solution.py:403
  18.6 7.0 %collective-permute-start = (f32[96,128]{1,0:T(8,128)S(1)}, f32[96,128]{1,0:T(8,128)S(1)}, u32[]{:S(2)}, u32[]{:S(2)}) collective-permute-start(f32[96,128]{1,0:T(8,128)S(1)} %get-tuple-element.12.after_ref.own_ref), channel_id=1, source_target_pairs={{0,16},{8,24},{16,0},{24,8},{32,48},{40,56},{48,32},{56,40},{64,80... | collective-permute-start | bytes 147464 | tf_op jit(solution)/shard_map/ppermute | solution.py:398
  25.6 0.0 copy-done.2
  25.6 0.1 copy.10.links_ref
  25.7 0.0 copy-done.1
  25.7 0.0 copy-done
  25.7 0.2 shard_map.75.after_ref.inner_ref
  26.0 0.0 all-to-all-done.slots_ref
  26.0 1.0 %shard_map.74 = (f32[4,8,128]{2,1,0:T(8,128)S(1)}, f32[16,128]{1,0:T(8,128)S(1)}) custom-call(f32[12,24,128]{2,1,0:T(8,128)S(1)} %all-to-all-done.slots_ref, s32[6,4,3]{2,1,0:T(4,128)S(1)} %copy.10.links_ref), custom_call_target="tpu_custom_call" | custom-call | tf_op jit(solution)/shard_map/pallas_call | solution.py:404
  27.0 3.1 %collective-permute-done.other_ref = f32[96,128]{1,0:T(8,128)S(1)} collective-permute-done((f32[96,128]{1,0:T(8,128)S(1)}, f32[96,128]{1,0:T(8,128)S(1)}, u32[]{:S(2)}, u32[]{:S(2)}) %collective-permute-start) | collective-permute-done | bytes 49184 | tf_op jit(solution)/shard_map/ppermute | solution.py:398
  30.1 0.1 shard_map.76
  30.2 8.7 %all_to_all.10.slot_ref = f32[4,192,128]{2,1,0:T(8,128)S(1)} all-to-all(f32[4,192,128]{2,1,0:T(8,128)S(1)} %shard_map.76), channel_id=1, replica_groups={{64,96,0,32},{72,104,8,40},{80,112,16,48},{88,120,24,56},{65,97,1,33},{..., dimensions={0} | all-to-all | bytes 786432 | tf_op jit(solution)/shard_map/all_to_all | solution.py:427
  38.9 5.3 %collective-permute-start.1 = (f32[4,192,128]{2,1,0:T(8,128)S(1)}, f32[4,192,128]{2,1,0:T(8,128)S(1)}, u32[]{:S(2)}, u32[]{:S(2)}) collective-permute-start(f32[4,192,128]{2,1,0:T(8,128)S(1)} %all_to_all.10.slot_ref), channel_id=1, source_target_pairs={{0,8},{8,0},{16,24},{24,16},{32,40},{40,32},{48,56},{56,48},{64,72... | collective-permute-start | bytes 1179656 | tf_op jit(solution)/shard_map/ppermute | solution.py:428
  44.2 1.1 %shard_map.77 = (f32[5,32,512]{2,1,0:T(8,128)S(1)}, f32[24,128]{1,0:T(8,128)S(1)}) custom-call(f32[4,192,128]{2,1,0:T(8,128)S(1)} %all_to_all.10.slot_ref, f32[4,32,512]{2,1,0:T(8,128)S(1)} %shard_map.75.after_ref.inner_ref, f32[16,128]{1,0:T(8,128)S(1)} %get-tuple-element.16.ends_ref.end_ref), custom_call_target="tpu_custom_call" | custom-call | flops 1048576 | bytes 1048576 | tf_op jit(solution)/shard_map/pallas_call | solution.py:436
  45.4 0.2 collective-permute-done.1.slot_ref
  45.6 2.2 %shard_map.78 = f32[4,32,512]{2,1,0:T(8,128)} custom-call(f32[4,192,128]{2,1,0:T(8,128)S(1)} %collective-permute-done.1.slot_ref, f32[5,32,512]{2,1,0:T(8,128)S(1)} %get-tuple-element.17.near_ref, f32[24,128]{1,0:T(8,128)S(1)} %get-tuple-element.18.halo_ref, f32[3,32,512]{2,1,0:T(8,128)S(1)} %bitcast.17), custom_call_target="tpu_custom_call" | custom-call | tf_op jit(solution)/shard_map/pallas_call | solution.py:445
Async XLA Ops:
  0.0 25.7 %copy-start.1 = (f32[1,1,3,32,512]{4,3,2,1,0:T(8,128)S(1)}, f32[1,1,3,32,512]{4,3,2,1,0:T(8,128)}, u32[]{:S(2)}) copy-start(f32[1,1,3,32,512]{4,3,2,1,0:T(8,128)} %param.8) | copy-start | bytes 589828
  1.8 23.9 %copy-start = (f32[1,1,4,32,512]{4,3,2,1,0:T(8,128)S(1)}, f32[1,1,4,32,512]{4,3,2,1,0:T(8,128)}, u32[]{:S(2)}) copy-start(f32[1,1,4,32,512]{4,3,2,1,0:T(8,128)} %param.7) | copy-start | bytes 786436
  1.8 23.8 %copy-start.2 = (s32[6,4,3]{0,1,2:T(4,128)S(1)}, s32[6,4,3]{0,1,2:T(4,128)}, u32[]{:S(2)}) copy-start(s32[6,4,3]{0,1,2:T(4,128)} %param.9) | copy-start | bytes 868
  1.8 24.1 %all-to-all-start = ((f32[12,24,128]{2,1,0:T(8,128)}), f32[12,24,128]{2,1,0:T(8,128)S(1)}, u32[]{:S(2)}, u32[]{:S(2)}) async-start(f32[12,24,128]{2,1,0:T(8,128)} %get-tuple-element.14), calls=%async_computation | async-start | bytes 294912 | tf_op jit(solution)/shard_map/all_to_all | solution.py:403
  18.6 11.5 %collective-permute-start = (f32[96,128]{1,0:T(8,128)S(1)}, f32[96,128]{1,0:T(8,128)S(1)}, u32[]{:S(2)}, u32[]{:S(2)}) collective-permute-start(f32[96,128]{1,0:T(8,128)S(1)} %get-tuple-element.12.after_ref.own_ref), channel_id=1, source_target_pairs={{0,16},{8,24},{16,0},{24,8},{32,48},{40,56},{48,32},{56,40},{64,80... | collective-permute-start | bytes 147464 | tf_op jit(solution)/shard_map/ppermute | solution.py:398
  38.9 6.6 %collective-permute-start.1 = (f32[4,192,128]{2,1,0:T(8,128)S(1)}, f32[4,192,128]{2,1,0:T(8,128)S(1)}, u32[]{:S(2)}, u32[]{:S(2)}) collective-permute-start(f32[4,192,128]{2,1,0:T(8,128)S(1)} %all_to_all.10.slot_ref), channel_id=1, source_target_pairs={{0,8},{8,0},{16,24},{24,16},{32,40},{40,32},{48,56},{56,48},{64,72... | collective-permute-start | bytes 1179656 | tf_op jit(solution)/shard_map/ppermute | solution.py:428

commit v5 on v4

--- a/solution.py
+++ b/solution.py
@@ -256,32 +256,29 @@
     return jnp.concatenate([from_free(sides), ends], 0)
 
 
-def deposit_start(slot_ref, total_ref, meta_ref, corner_ref, sem):
+def deposit(slot_ref, total_ref):
     first_row = 32 * lax.axis_index("tile")
-    meta = jnp.concatenate([slot_ref[i // 2, OWN * (i % 2) : OWN * (i % 2) + 2, :] for i in range(8)], 0)
-    meta = meta.astype(jnp.int32)
-    r = (meta >> 9) - first_row
-    meta_ref[...] = jnp.where((r > -(WIN + 1)) & (r < 32), meta, -1)
-    copy = pltpu.make_async_copy(meta_ref, corner_ref, sem)
-    copy.start()
+    heads = [
+        jnp.concatenate([slot_ref[i // 2, OWN * (i % 2) + e : OWN * (i % 2) + e + 1, :] for i in range(8)], 0)
+        for e in range(2)
+    ]
+    lane = iota((8, 128), 1)
+    meta = jnp.where(lane < META + 2, heads[0], pltpu.roll(heads[1], 2, 1))
+    corner = meta.astype(jnp.int32)
+    r = (corner >> 9) - first_row
+    hit = (lane >= META) & (lane < META + 4) & (r > -(WIN + 1)) & (r < 32)
+    keys = jnp.where(hit, corner * 32 + 4 * iota((8, 128), 0) + lane - META, -1).astype(jnp.float32)
     total_ref[:, 16:56, :] = jnp.zeros((5, 40, 640), jnp.float32)
-    return copy
-
-
-def deposit(slot_ref, total_ref, corner_ref, list_ref):
-    first_row = 32 * lax.axis_index("tile")
-    count = jnp.int32(0)
-    for i in range(32):
-        corner = corner_ref[i // 2, META + i % 2]
-        list_ref[0, count] = corner
-        list_ref[1, count] = i
-        count = count + jnp.where(corner >= 0, 1, 0)
     lane = iota((32, 128), 1)
     sub = iota((32, 128), 0)
 
-    def one(n, carry):
-        corner = list_ref[0, n]
-        i = list_ref[1, n]
+    def one(carry):
+        left, top = carry
+        left = jnp.where(left == top, -1.0, left)
+        following = jnp.max(left)
+        key = top.astype(jnp.int32)
+        corner = key >> 5
+        i = key & 31
         at = (corner >> 9) - first_row + 24
         b = corner & 511
         off = b & 127
@@ -300,9 +297,9 @@
             moved = pltpu.roll(window, (off - WIN * m + 128) % 128, 1)
             total_ref[m, rows, here] += jnp.where(low_side, moved, 0.0)
             total_ref[m, rows, there] += jnp.where(high_side, moved, 0.0)
-        return carry
-
-    lax.fori_loop(0, count, one, 0)
+        return left, following
+
+    lax.while_loop(lambda carry: carry[1] >= 0.0, one, (keys, jnp.max(keys)))
 
 
 def deposited(total_ref, m):
@@ -311,22 +308,19 @@
     return jnp.concatenate([mass[:, 0:128] + spill, mass[:, 128:512]], 1)
 
 
-def near_kernel(slot_ref, inner_ref, end_ref, out_ref, halo_ref, total_ref, meta_ref, corner_ref, list_ref, sem):
+def near_kernel(slot_ref, inner_ref, end_ref, out_ref, halo_ref, total_ref):
     _, x, z, c = place_of()
-    copy = deposit_start(slot_ref, total_ref, meta_ref, corner_ref, sem)
     halo = halo_sum(slot_ref, lax.rem(x + 4 - XLEAD, 4))
     halo_ref[0:8] = halo[0:8]
     halo_ref[8:24] = halo[8:24] + jnp.where((x == 3 * z) & (c == z), end_ref[...], 0.0)
-    copy.wait()
-    deposit(slot_ref, total_ref, corner_ref, list_ref)
+    deposit(slot_ref, total_ref)
     for m in range(4):
         out_ref[m] = inner_ref[m] + deposited(total_ref, m)
     out_ref[4] = 1.0 + deposited(total_ref, 4)
 
 
-def final_kernel(slot_ref, near_ref, halo_ref, courant_ref, out_ref, total_ref, meta_ref, corner_ref, list_ref, sem):
+def final_kernel(slot_ref, near_ref, halo_ref, courant_ref, out_ref, total_ref):
     _, x, z, c = place_of()
-    copy = deposit_start(slot_ref, total_ref, meta_ref, corner_ref, sem)
     halo = halo_ref[...] + halo_sum(slot_ref, -1)
     chip = lax.rem(x + 4 - XLEAD, 4)
     kept = from_free([slot_ref[chip, WROWS * w : WROWS * w + 16, :] for w in range(8)])
@@ -354,8 +348,7 @@
         left = value[:, 0:128] + first * west[32 * m : 32 * m + 32]
         right = value[:, 384:512] + last * east[32 * m : 32 * m + 32]
         out_ref[m] = jnp.concatenate([left, value[:, 128:384], right], 1)
-    copy.wait()
-    deposit(slot_ref, total_ref, corner_ref, list_ref)
+    deposit(slot_ref, total_ref)
     scale = 1.0 / (near_ref[4] + deposited(total_ref, 4))
     for m in range(4):
         out_ref[m] = (out_ref[m] + deposited(total_ref, m)) * scale
@@ -426,13 +419,7 @@
     chips = [[tile_of((XLEAD + j) % 4, z, c) for j in range(4)] for z in range(2) for c in range(2)]
     near = lax.all_to_all(packed, "tile", 0, 0, tiled=True, axis_index_groups=chips)
     far = lax.ppermute(near, "tile", [(t, t ^ 1) for t in range(16)])
-    scratch = [
-        pltpu.VMEM((5, 88, 640), jnp.float32),
-        pltpu.VMEM((16, 128), jnp.int32),
-        pltpu.SMEM((16, 128), jnp.int32),
-        pltpu.SMEM((2, 40), jnp.int32),
-        pltpu.SemaphoreType.DMA,
-    ]
+    scratch = [pltpu.VMEM((5, 88, 640), jnp.float32)]
     summed, halo = pl.pallas_call(
         near_kernel,
         out_shape=(shape(5, 32, 512), shape(24, 128)),

time: 48 us -> 47.1 us (0.981)
  Pallas kernels: 6.48 us -> 5.32 us
    pallas_call x1, Pallas kernels: 2.18 us -> 1.27 us  [body(): pl.pallas_call(final_kernel, out_shape=shape(4, 32, 512), in_specs=[VMEM,...]
where the time goes in v5:
time: 47.1 us; the launch traced here: 46.8 us
  starting transfers between devices  29.1 us (62%)
  blocking collectives  8.68 us (18%)
  Pallas kernels  5.32 us (11%)
  waiting for transfers between devices  3.55 us (8%)
    all_to_all x1, starting transfers between devices, body(): lax.all_to_all(slots, ('panel', 'tile'), 0, 0, tiled=True, axis_index_gro...  16.7 us
    all_to_all x1, blocking collectives, body(): lax.all_to_all(packed, 'tile', 0, 0, tiled=True, axis_index_groups=chips)  8.68 us
    ppermute x1, starting transfers between devices, body(): other = lax.ppermute(own, 'tile', [(t, t ^ 2) for t in range(16)])  7.03 us
    ppermute x1, starting transfers between devices, body(): far = lax.ppermute(near, 'tile', [(t, t ^ 1) for t in range(16)])  5.31 us
    ppermute x1, waiting for transfers between devices, body(): other = lax.ppermute(own, 'tile', [(t, t ^ 2) for t in range(16)])  3.09 us
    pallas_call x1, Pallas kernels, body(): pl.pallas_call(pool_kernel, out_shape=(shape(OWN, 128), shape(12, 24, 128...  1.81 us
    pallas_call x1, Pallas kernels, body(): pl.pallas_call(final_kernel, out_shape=shape(4, 32, 512), in_specs=[VMEM,...  1.27 us
    pallas_call x1, Pallas kernels, body(): pl.pallas_call(lines_kernel, out_shape=(shape(4, 8, 128), shape(16, 128))...  1.03 us
  transfers between devices with their start and end apart: 3, of which 2 were waited for; matrix products, arithmetic and copies ran while one was open for 0% of the time, Pallas kernels for 5%

profile of v5, /device:TPU:1, one launch (start us, length us, event | category | flops | bytes accessed | tf_op | source)
XLA Modules:
  0.0 46.8 jit_solution(9065248273230725692)
XLA Ops:
  0.0 0.0 copy-start.1
  0.0 1.8 %shard_map.73 = (f32[96,128]{1,0:T(8,128)S(1)}, f32[12,24,128]{2,1,0:T(8,128)}, f32[16,128]{1,0:T(8,128)S(1)}) custom-call(f32[4,128,128]{2,1,0:T(8,128)} %bitcast.18, f32[128,128]{1,0:T(8,128)} %bitcast.19, s32[4,4096]{1,0:T(4,128)} %bitcast.20, f32[4,32,512]{2,1,0:T(8,128)} %bitcast.14, s32[1,4]{1,0:T(1,128)} %live_hbm.1), custom_call_target="tpu_custom_call" | custom-call | tf_op jit(solution)/shard_map/pallas_call | solution.py:375
  1.8 0.0 copy-start
  1.8 0.0 copy-start.2
  1.8 16.7 %all-to-all-start = ((f32[12,24,128]{2,1,0:T(8,128)}), f32[12,24,128]{2,1,0:T(8,128)S(1)}, u32[]{:S(2)}, u32[]{:S(2)}) async-start(f32[12,24,128]{2,1,0:T(8,128)} %get-tuple-element.14), calls=%async_computation | async-start | bytes 294912 | tf_op jit(solution)/shard_map/all_to_all | solution.py:396
  18.6 7.0 %collective-permute-start = (f32[96,128]{1,0:T(8,128)S(1)}, f32[96,128]{1,0:T(8,128)S(1)}, u32[]{:S(2)}, u32[]{:S(2)}) collective-permute-start(f32[96,128]{1,0:T(8,128)S(1)} %get-tuple-element.12.after_ref.own_ref), channel_id=1, source_target_pairs={{0,16},{8,24},{16,0},{24,8},{32,48},{40,56},{48,32},{56,40},{64,80... | collective-permute-start | bytes 147464 | tf_op jit(solution)/shard_map/ppermute | solution.py:391
  25.6 0.0 copy-done.2
  25.6 0.1 copy.10.links_ref
  25.7 0.0 copy-done.1
  25.7 0.0 copy-done
  25.7 0.2 shard_map.75.after_ref.inner_ref
  26.0 0.0 all-to-all-done.slots_ref
  26.0 1.0 %shard_map.74 = (f32[4,8,128]{2,1,0:T(8,128)S(1)}, f32[16,128]{1,0:T(8,128)S(1)}) custom-call(f32[12,24,128]{2,1,0:T(8,128)S(1)} %all-to-all-done.slots_ref, s32[6,4,3]{2,1,0:T(4,128)S(1)} %copy.10.links_ref), custom_call_target="tpu_custom_call" | custom-call | tf_op jit(solution)/shard_map/pallas_call | solution.py:397
  27.0 3.1 %collective-permute-done.other_ref = f32[96,128]{1,0:T(8,128)S(1)} collective-permute-done((f32[96,128]{1,0:T(8,128)S(1)}, f32[96,128]{1,0:T(8,128)S(1)}, u32[]{:S(2)}, u32[]{:S(2)}) %collective-permute-start) | collective-permute-done | bytes 49184 | tf_op jit(solution)/shard_map/ppermute | solution.py:391
  30.1 0.1 shard_map.76
  30.2 8.7 %all_to_all.10.slot_ref = f32[4,192,128]{2,1,0:T(8,128)S(1)} all-to-all(f32[4,192,128]{2,1,0:T(8,128)S(1)} %shard_map.76), channel_id=1, replica_groups={{64,96,0,32},{72,104,8,40},{80,112,16,48},{88,120,24,56},{65,97,1,33},{..., dimensions={0} | all-to-all | bytes 786432 | tf_op jit(solution)/shard_map/all_to_all | solution.py:420
  38.9 5.3 %collective-permute-start.1 = (f32[4,192,128]{2,1,0:T(8,128)S(1)}, f32[4,192,128]{2,1,0:T(8,128)S(1)}, u32[]{:S(2)}, u32[]{:S(2)}) collective-permute-start(f32[4,192,128]{2,1,0:T(8,128)S(1)} %all_to_all.10.slot_ref), channel_id=1, source_target_pairs={{0,8},{8,0},{16,24},{24,16},{32,40},{40,32},{48,56},{56,48},{64,72... | collective-permute-start | bytes 1179656 | tf_op jit(solution)/shard_map/ppermute | solution.py:421
  44.2 0.9 %shard_map.77 = (f32[5,32,512]{2,1,0:T(8,128)S(1)}, f32[24,128]{1,0:T(8,128)S(1)}) custom-call(f32[4,192,128]{2,1,0:T(8,128)S(1)} %all_to_all.10.slot_ref, f32[4,32,512]{2,1,0:T(8,128)S(1)} %shard_map.75.after_ref.inner_ref, f32[16,128]{1,0:T(8,128)S(1)} %get-tuple-element.16.ends_ref.end_ref), custom_call_target="tpu_custom_call" | custom-call | flops 1048576 | bytes 1048576 | tf_op jit(solution)/shard_map/pallas_call | solution.py:423
  45.1 0.5 collective-permute-done.1.slot_ref
  45.6 1.3 %shard_map.78 = f32[4,32,512]{2,1,0:T(8,128)} custom-call(f32[4,192,128]{2,1,0:T(8,128)S(1)} %collective-permute-done.1.slot_ref, f32[5,32,512]{2,1,0:T(8,128)S(1)} %get-tuple-element.17.near_ref, f32[24,128]{1,0:T(8,128)S(1)} %get-tuple-element.18.halo_ref, f32[3,32,512]{2,1,0:T(8,128)S(1)} %bitcast.17), custom_call_target="tpu_custom_call" | custom-call | tf_op jit(solution)/shard_map/pallas_call | solution.py:432
Async XLA Ops:
  0.0 25.7 %copy-start.1 = (f32[1,1,3,32,512]{4,3,2,1,0:T(8,128)S(1)}, f32[1,1,3,32,512]{4,3,2,1,0:T(8,128)}, u32[]{:S(2)}) copy-start(f32[1,1,3,32,512]{4,3,2,1,0:T(8,128)} %param.8) | copy-start | bytes 589828
  1.8 23.9 %copy-start = (f32[1,1,4,32,512]{4,3,2,1,0:T(8,128)S(1)}, f32[1,1,4,32,512]{4,3,2,1,0:T(8,128)}, u32[]{:S(2)}) copy-start(f32[1,1,4,32,512]{4,3,2,1,0:T(8,128)} %param.7) | copy-start | bytes 786436
  1.8 23.8 %copy-start.2 = (s32[6,4,3]{0,1,2:T(4,128)S(1)}, s32[6,4,3]{0,1,2:T(4,128)}, u32[]{:S(2)}) copy-start(s32[6,4,3]{0,1,2:T(4,128)} %param.9) | copy-start | bytes 868
  1.8 24.1 %all-to-all-start = ((f32[12,24,128]{2,1,0:T(8,128)}), f32[12,24,128]{2,1,0:T(8,128)S(1)}, u32[]{:S(2)}, u32[]{:S(2)}) async-start(f32[12,24,128]{2,1,0:T(8,128)} %get-tuple-element.14), calls=%async_computation | async-start | bytes 294912 | tf_op jit(solution)/shard_map/all_to_all | solution.py:396
  18.6 11.5 %collective-permute-start = (f32[96,128]{1,0:T(8,128)S(1)}, f32[96,128]{1,0:T(8,128)S(1)}, u32[]{:S(2)}, u32[]{:S(2)}) collective-permute-start(f32[96,128]{1,0:T(8,128)S(1)} %get-tuple-element.12.after_ref.own_ref), channel_id=1, source_target_pairs={{0,16},{8,24},{16,0},{24,8},{32,48},{40,56},{48,32},{56,40},{64,80... | collective-permute-start | bytes 147464 | tf_op jit(solution)/shard_map/ppermute | solution.py:391
  38.9 6.6 %collective-permute-start.1 = (f32[4,192,128]{2,1,0:T(8,128)S(1)}, f32[4,192,128]{2,1,0:T(8,128)S(1)}, u32[]{:S(2)}, u32[]{:S(2)}) collective-permute-start(f32[4,192,128]{2,1,0:T(8,128)S(1)} %all_to_all.10.slot_ref), channel_id=1, source_target_pairs={{0,8},{8,0},{16,24},{24,16},{32,40},{40,32},{48,56},{56,48},{64,72... | collective-permute-start | bytes 1179656 | tf_op jit(solution)/shard_map/ppermute | solution.py:421

commit v6 on v5

--- a/solution.py
+++ b/solution.py
@@ -290,13 +290,19 @@
         q = (b >> 7) * 128
         here = pl.ds(pl.multiple_of(q, 128), 128)
         there = pl.ds(pl.multiple_of(q + 128, 128), 128)
-        inside = (sub >= turn) & (sub < turn + WIN)
-        low_side = inside & (lane >= off) & (lane < off + WIN)
-        high_side = inside & (lane < off + WIN - 128)
+        window = jnp.where((sub >= turn) & (sub < turn + WIN), window, 0.0)
+        low_side = (lane >= off) & (lane < off + WIN)
+        high_side = lane < off + WIN - 128
         for m in range(5):
             moved = pltpu.roll(window, (off - WIN * m + 128) % 128, 1)
             total_ref[m, rows, here] += jnp.where(low_side, moved, 0.0)
-            total_ref[m, rows, there] += jnp.where(high_side, moved, 0.0)
+
+        @pl.when(off > 128 - WIN)
+        def _():
+            for m in range(5):
+                moved = pltpu.roll(window, (off - WIN * m + 128) % 128, 1)
+                total_ref[m, rows, there] += jnp.where(high_side, moved, 0.0)
+
         return left, following
 
     lax.while_loop(lambda carry: carry[1] >= 0.0, one, (keys, jnp.max(keys)))

time: 47.1 us -> 47.1 us (level)
  transfers between devices with their start and end apart: 3 -> 3, of which waited for: 2 -> 2; matrix products, arithmetic and copies ran while one was open for 0% -> 0% of each run, Pallas kernels for 5% -> 4%
where the time goes in v6:
time: 47.1 us; the launch traced here: 46.8 us
  starting transfers between devices  29.1 us (62%)
  blocking collectives  8.68 us (18%)
  Pallas kernels  4.87 us (10%)
  waiting for transfers between devices  3.93 us (8%)
    all_to_all x1, starting transfers between devices, body(): lax.all_to_all(slots, ('panel', 'tile'), 0, 0, tiled=True, axis_index_gro...  16.7 us
    all_to_all x1, blocking collectives, body(): lax.all_to_all(packed, 'tile', 0, 0, tiled=True, axis_index_groups=chips)  8.68 us
    ppermute x1, starting transfers between devices, body(): other = lax.ppermute(own, 'tile', [(t, t ^ 2) for t in range(16)])  7.03 us
    ppermute x1, starting transfers between devices, body(): far = lax.ppermute(near, 'tile', [(t, t ^ 1) for t in range(16)])  5.31 us
    ppermute x1, waiting for transfers between devices, body(): other = lax.ppermute(own, 'tile', [(t, t ^ 2) for t in range(16)])  3.09 us
    pallas_call x1, Pallas kernels, body(): pl.pallas_call(pool_kernel, out_shape=(shape(OWN, 128), shape(12, 24, 128...  1.81 us
    pallas_call x1, Pallas kernels, body(): pl.pallas_call(final_kernel, out_shape=shape(4, 32, 512), in_specs=[VMEM,...  1.21 us
    pallas_call x1, Pallas kernels, body(): pl.pallas_call(lines_kernel, out_shape=(shape(4, 8, 128), shape(16, 128))...  1.03 us
  transfers between devices with their start and end apart: 3, of which 2 were waited for; matrix products, arithmetic and copies ran while one was open for 0% of the time, Pallas kernels for 4%

profile of v6, /device:TPU:1, one launch (start us, length us, event | category | flops | bytes accessed | tf_op | source)
XLA Modules:
  0.0 46.8 jit_solution(1364967642875130866)
XLA Ops:
  0.0 0.0 copy-start.1
  0.0 1.8 %shard_map.73 = (f32[96,128]{1,0:T(8,128)S(1)}, f32[12,24,128]{2,1,0:T(8,128)}, f32[16,128]{1,0:T(8,128)S(1)}) custom-call(f32[4,128,128]{2,1,0:T(8,128)} %bitcast.18, f32[128,128]{1,0:T(8,128)} %bitcast.19, s32[4,4096]{1,0:T(4,128)} %bitcast.20, f32[4,32,512]{2,1,0:T(8,128)} %bitcast.14, s32[1,4]{1,0:T(1,128)} %live_hbm.1), custom_call_target="tpu_custom_call" | custom-call | tf_op jit(solution)/shard_map/pallas_call | solution.py:381
  1.8 0.0 copy-start
  1.8 0.0 copy-start.2
  1.8 16.7 %all-to-all-start = ((f32[12,24,128]{2,1,0:T(8,128)}), f32[12,24,128]{2,1,0:T(8,128)S(1)}, u32[]{:S(2)}, u32[]{:S(2)}) async-start(f32[12,24,128]{2,1,0:T(8,128)} %get-tuple-element.14), calls=%async_computation | async-start | bytes 294912 | tf_op jit(solution)/shard_map/all_to_all | solution.py:402
  18.6 7.0 %collective-permute-start = (f32[96,128]{1,0:T(8,128)S(1)}, f32[96,128]{1,0:T(8,128)S(1)}, u32[]{:S(2)}, u32[]{:S(2)}) collective-permute-start(f32[96,128]{1,0:T(8,128)S(1)} %get-tuple-element.12.after_ref.own_ref), channel_id=1, source_target_pairs={{0,16},{8,24},{16,0},{24,8},{32,48},{40,56},{48,32},{56,40},{64,80... | collective-permute-start | bytes 147464 | tf_op jit(solution)/shard_map/ppermute | solution.py:397
  25.6 0.0 copy-done.2
  25.6 0.1 copy.10.links_ref
  25.7 0.0 copy-done.1
  25.7 0.0 copy-done
  25.7 0.2 shard_map.75.after_ref.inner_ref
  26.0 0.0 all-to-all-done.slots_ref
  26.0 1.0 %shard_map.74 = (f32[4,8,128]{2,1,0:T(8,128)S(1)}, f32[16,128]{1,0:T(8,128)S(1)}) custom-call(f32[12,24,128]{2,1,0:T(8,128)S(1)} %all-to-all-done.slots_ref, s32[6,4,3]{2,1,0:T(4,128)S(1)} %copy.10.links_ref), custom_call_target="tpu_custom_call" | custom-call | tf_op jit(solution)/shard_map/pallas_call | solution.py:403
  27.0 3.1 %collective-permute-done.other_ref = f32[96,128]{1,0:T(8,128)S(1)} collective-permute-done((f32[96,128]{1,0:T(8,128)S(1)}, f32[96,128]{1,0:T(8,128)S(1)}, u32[]{:S(2)}, u32[]{:S(2)}) %collective-permute-start) | collective-permute-done | bytes 49184 | tf_op jit(solution)/shard_map/ppermute | solution.py:397
  30.1 0.1 shard_map.76
  30.2 8.7 %all_to_all.10.slot_ref = f32[4,192,128]{2,1,0:T(8,128)S(1)} all-to-all(f32[4,192,128]{2,1,0:T(8,128)S(1)} %shard_map.76), channel_id=1, replica_groups={{64,96,0,32},{72,104,8,40},{80,112,16,48},{88,120,24,56},{65,97,1,33},{..., dimensions={0} | all-to-all | bytes 786432 | tf_op jit(solution)/shard_map/all_to_all | solution.py:426
  38.9 5.3 %collective-permute-start.1 = (f32[4,192,128]{2,1,0:T(8,128)S(1)}, f32[4,192,128]{2,1,0:T(8,128)S(1)}, u32[]{:S(2)}, u32[]{:S(2)}) collective-permute-start(f32[4,192,128]{2,1,0:T(8,128)S(1)} %all_to_all.10.slot_ref), channel_id=1, source_target_pairs={{0,8},{8,0},{16,24},{24,16},{32,40},{40,32},{48,56},{56,48},{64,72... | collective-permute-start | bytes 1179656 | tf_op jit(solution)/shard_map/ppermute | solution.py:427
  44.2 0.5 %shard_map.77 = (f32[5,32,512]{2,1,0:T(8,128)S(1)}, f32[24,128]{1,0:T(8,128)S(1)}) custom-call(f32[4,192,128]{2,1,0:T(8,128)S(1)} %all_to_all.10.slot_ref, f32[4,32,512]{2,1,0:T(8,128)S(1)} %shard_map.75.after_ref.inner_ref, f32[16,128]{1,0:T(8,128)S(1)} %get-tuple-element.16.ends_ref.end_ref), custom_call_target="tpu_custom_call" | custom-call | flops 1048576 | bytes 1048576 | tf_op jit(solution)/shard_map/pallas_call | solution.py:429
  44.7 0.8 %collective-permute-done.1.slot_ref = f32[4,192,128]{2,1,0:T(8,128)S(1)} collective-permute-done((f32[4,192,128]{2,1,0:T(8,128)S(1)}, f32[4,192,128]{2,1,0:T(8,128)S(1)}, u32[]{:S(2)}, u32[]{:S(2)}) %collective-permute-start.1) | collective-permute-done | bytes 393248 | tf_op jit(solution)/shard_map/ppermute | solution.py:427
  45.6 1.2 %shard_map.78 = f32[4,32,512]{2,1,0:T(8,128)} custom-call(f32[4,192,128]{2,1,0:T(8,128)S(1)} %collective-permute-done.1.slot_ref, f32[5,32,512]{2,1,0:T(8,128)S(1)} %get-tuple-element.17.near_ref, f32[24,128]{1,0:T(8,128)S(1)} %get-tuple-element.18.halo_ref, f32[3,32,512]{2,1,0:T(8,128)S(1)} %bitcast.17), custom_call_target="tpu_custom_call" | custom-call | tf_op jit(solution)/shard_map/pallas_call | solution.py:438
Async XLA Ops:
  0.0 25.7 %copy-start.1 = (f32[1,1,3,32,512]{4,3,2,1,0:T(8,128)S(1)}, f32[1,1,3,32,512]{4,3,2,1,0:T(8,128)}, u32[]{:S(2)}) copy-start(f32[1,1,3,32,512]{4,3,2,1,0:T(8,128)} %param.8) | copy-start | bytes 589828
  1.8 23.9 %copy-start = (f32[1,1,4,32,512]{4,3,2,1,0:T(8,128)S(1)}, f32[1,1,4,32,512]{4,3,2,1,0:T(8,128)}, u32[]{:S(2)}) copy-start(f32[1,1,4,32,512]{4,3,2,1,0:T(8,128)} %param.7) | copy-start | bytes 786436
  1.8 23.8 %copy-start.2 = (s32[6,4,3]{0,1,2:T(4,128)S(1)}, s32[6,4,3]{0,1,2:T(4,128)}, u32[]{:S(2)}) copy-start(s32[6,4,3]{0,1,2:T(4,128)} %param.9) | copy-start | bytes 868
  1.8 24.1 %all-to-all-start = ((f32[12,24,128]{2,1,0:T(8,128)}), f32[12,24,128]{2,1,0:T(8,128)S(1)}, u32[]{:S(2)}, u32[]{:S(2)}) async-start(f32[12,24,128]{2,1,0:T(8,128)} %get-tuple-element.14), calls=%async_computation | async-start | bytes 294912 | tf_op jit(solution)/shard_map/all_to_all | solution.py:402
  18.6 11.5 %collective-permute-start = (f32[96,128]{1,0:T(8,128)S(1)}, f32[96,128]{1,0:T(8,128)S(1)}, u32[]{:S(2)}, u32[]{:S(2)}) collective-permute-start(f32[96,128]{1,0:T(8,128)S(1)} %get-tuple-element.12.after_ref.own_ref), channel_id=1, source_target_pairs={{0,16},{8,24},{16,0},{24,8},{32,48},{40,56},{48,32},{56,40},{64,80... | collective-permute-start | bytes 147464 | tf_op jit(solution)/shard_map/ppermute | solution.py:397
  38.9 6.6 %collective-permute-start.1 = (f32[4,192,128]{2,1,0:T(8,128)S(1)}, f32[4,192,128]{2,1,0:T(8,128)S(1)}, u32[]{:S(2)}, u32[]{:S(2)}) collective-permute-start(f32[4,192,128]{2,1,0:T(8,128)S(1)} %all_to_all.10.slot_ref), channel_id=1, source_target_pairs={{0,8},{8,0},{16,24},{24,16},{32,40},{40,32},{48,56},{56,48},{64,72... | collective-permute-start | bytes 1179656 | tf_op jit(solution)/shard_map/ppermute | solution.py:427

commit v7 on v6

--- a/solution.py
+++ b/solution.py
@@ -12,7 +12,7 @@
 SLOT = 2 * OWN
 META = 110
 FREE = 112
-LEAD = 10
+LEAD = 11
 XLEAD = 2
 VMEM = pl.BlockSpec(memory_space=pltpu.VMEM)
 SMEM = pl.BlockSpec(memory_space=pltpu.SMEM)

time: 47.1 us -> 47 us (level)
  waiting for transfers between devices: 3.93 us -> 3.22 us
  Pallas kernels: 4.87 us -> 5.35 us
    ppermute x1, starting transfers between devices: 7.03 us -> 7.93 us  [body(): other = lax.ppermute(own, 'tile', [(t, t ^ 2) for t in range(16)])]
    ppermute x1, starting transfers between devices: 5.31 us -> 4.41 us  [body(): far = lax.ppermute(near, 'tile', [(t, t ^ 1) for t in range(16)])]
    ppermute x1, waiting for transfers between devices: 3.09 us -> 2.62 us  [body(): other = lax.ppermute(own, 'tile', [(t, t ^ 2) for t in range(16)])]
where the time goes in v7:
time: 47 us; the launch traced here: 46.8 us
  starting transfers between devices  29.1 us (62%)
  blocking collectives  8.97 us (19%)
  Pallas kernels  5.35 us (11%)
  waiting for transfers between devices  3.22 us (7%)
    all_to_all x1, starting transfers between devices, body(): lax.all_to_all(slots, ('panel', 'tile'), 0, 0, tiled=True, axis_index_gro...  16.7 us
    all_to_all x1, blocking collectives, body(): lax.all_to_all(packed, 'tile', 0, 0, tiled=True, axis_index_groups=chips)  8.97 us
    ppermute x1, starting transfers between devices, body(): other = lax.ppermute(own, 'tile', [(t, t ^ 2) for t in range(16)])  7.93 us
    ppermute x1, starting transfers between devices, body(): far = lax.ppermute(near, 'tile', [(t, t ^ 1) for t in range(16)])  4.41 us
    ppermute x1, waiting for transfers between devices, body(): other = lax.ppermute(own, 'tile', [(t, t ^ 2) for t in range(16)])  2.62 us
    pallas_call x1, Pallas kernels, body(): pl.pallas_call(pool_kernel, out_shape=(shape(OWN, 128), shape(12, 24, 128...  1.81 us
    pallas_call x1, Pallas kernels, body(): pl.pallas_call(final_kernel, out_shape=shape(4, 32, 512), in_specs=[VMEM,...  1.45 us
    pallas_call x1, Pallas kernels, body(): pl.pallas_call(lines_kernel, out_shape=(shape(4, 8, 128), shape(16, 128))...  1.03 us
  transfers between devices with their start and end apart: 3, of which 2 were waited for; matrix products, arithmetic and copies ran while one was open for 0% of the time, Pallas kernels for 4%

profile of v7, /device:TPU:1, one launch (start us, length us, event | category | flops | bytes accessed | tf_op | source)
XLA Modules:
  0.0 46.8 jit_solution(14212419190732623678)
XLA Ops:
  0.0 0.0 copy-start.1
  0.0 1.8 %shard_map.73 = (f32[96,128]{1,0:T(8,128)S(1)}, f32[12,24,128]{2,1,0:T(8,128)}, f32[16,128]{1,0:T(8,128)S(1)}) custom-call(f32[4,128,128]{2,1,0:T(8,128)} %bitcast.18, f32[128,128]{1,0:T(8,128)} %bitcast.19, s32[4,4096]{1,0:T(4,128)} %bitcast.20, f32[4,32,512]{2,1,0:T(8,128)} %bitcast.14, s32[1,4]{1,0:T(1,128)} %live_hbm.1), custom_call_target="tpu_custom_call" | custom-call | tf_op jit(solution)/shard_map/pallas_call | solution.py:381
  1.8 0.0 copy-start
  1.8 0.0 copy-start.2
  1.8 16.7 %all-to-all-start = ((f32[12,24,128]{2,1,0:T(8,128)}), f32[12,24,128]{2,1,0:T(8,128)S(1)}, u32[]{:S(2)}, u32[]{:S(2)}) async-start(f32[12,24,128]{2,1,0:T(8,128)} %get-tuple-element.14), calls=%async_computation | async-start | bytes 294912 | tf_op jit(solution)/shard_map/all_to_all | solution.py:402
  18.6 7.9 %collective-permute-start = (f32[96,128]{1,0:T(8,128)S(1)}, f32[96,128]{1,0:T(8,128)S(1)}, u32[]{:S(2)}, u32[]{:S(2)}) collective-permute-start(f32[96,128]{1,0:T(8,128)S(1)} %get-tuple-element.12.after_ref.own_ref), channel_id=1, source_target_pairs={{0,16},{8,24},{16,0},{24,8},{32,48},{40,56},{48,32},{56,40},{64,80... | collective-permute-start | bytes 147464 | tf_op jit(solution)/shard_map/ppermute | solution.py:397
  26.5 0.0 copy-done.2
  26.5 0.1 copy.10.links_ref
  26.6 0.0 copy-done.1
  26.6 0.0 copy-done
  26.6 0.2 shard_map.75.after_ref.inner_ref
  26.9 0.0 all-to-all-done.slots_ref
  26.9 1.0 %shard_map.74 = (f32[4,8,128]{2,1,0:T(8,128)S(1)}, f32[16,128]{1,0:T(8,128)S(1)}) custom-call(f32[12,24,128]{2,1,0:T(8,128)S(1)} %all-to-all-done.slots_ref, s32[6,4,3]{2,1,0:T(4,128)S(1)} %copy.10.links_ref), custom_call_target="tpu_custom_call" | custom-call | tf_op jit(solution)/shard_map/pallas_call | solution.py:403
  27.9 2.6 %collective-permute-done.other_ref = f32[96,128]{1,0:T(8,128)S(1)} collective-permute-done((f32[96,128]{1,0:T(8,128)S(1)}, f32[96,128]{1,0:T(8,128)S(1)}, u32[]{:S(2)}, u32[]{:S(2)}) %collective-permute-start) | collective-permute-done | bytes 49184 | tf_op jit(solution)/shard_map/ppermute | solution.py:397
  30.5 0.1 shard_map.76
  30.7 9.0 %all_to_all.10.slot_ref = f32[4,192,128]{2,1,0:T(8,128)S(1)} all-to-all(f32[4,192,128]{2,1,0:T(8,128)S(1)} %shard_map.76), channel_id=1, replica_groups={{64,96,0,32},{72,104,8,40},{80,112,16,48},{88,120,24,56},{65,97,1,33},{..., dimensions={0} | all-to-all | bytes 786432 | tf_op jit(solution)/shard_map/all_to_all | solution.py:426
  39.6 4.4 %collective-permute-start.1 = (f32[4,192,128]{2,1,0:T(8,128)S(1)}, f32[4,192,128]{2,1,0:T(8,128)S(1)}, u32[]{:S(2)}, u32[]{:S(2)}) collective-permute-start(f32[4,192,128]{2,1,0:T(8,128)S(1)} %all_to_all.10.slot_ref), channel_id=1, source_target_pairs={{0,8},{8,0},{16,24},{24,16},{32,40},{40,32},{48,56},{56,48},{64,72... | collective-permute-start | bytes 1179656 | tf_op jit(solution)/shard_map/ppermute | solution.py:427
  44.1 0.7 %shard_map.77 = (f32[5,32,512]{2,1,0:T(8,128)S(1)}, f32[24,128]{1,0:T(8,128)S(1)}) custom-call(f32[4,192,128]{2,1,0:T(8,128)S(1)} %all_to_all.10.slot_ref, f32[4,32,512]{2,1,0:T(8,128)S(1)} %shard_map.75.after_ref.inner_ref, f32[16,128]{1,0:T(8,128)S(1)} %get-tuple-element.16.ends_ref.end_ref), custom_call_target="tpu_custom_call" | custom-call | flops 1048576 | bytes 1048576 | tf_op jit(solution)/shard_map/pallas_call | solution.py:429
  44.8 0.6 %collective-permute-done.1.slot_ref = f32[4,192,128]{2,1,0:T(8,128)S(1)} collective-permute-done((f32[4,192,128]{2,1,0:T(8,128)S(1)}, f32[4,192,128]{2,1,0:T(8,128)S(1)}, u32[]{:S(2)}, u32[]{:S(2)}) %collective-permute-start.1) | collective-permute-done | bytes 393248 | tf_op jit(solution)/shard_map/ppermute | solution.py:427
  45.4 1.4 %shard_map.78 = f32[4,32,512]{2,1,0:T(8,128)} custom-call(f32[4,192,128]{2,1,0:T(8,128)S(1)} %collective-permute-done.1.slot_ref, f32[5,32,512]{2,1,0:T(8,128)S(1)} %get-tuple-element.17.near_ref, f32[24,128]{1,0:T(8,128)S(1)} %get-tuple-element.18.halo_ref, f32[3,32,512]{2,1,0:T(8,128)S(1)} %bitcast.17), custom_call_target="tpu_custom_call" | custom-call | tf_op jit(solution)/shard_map/pallas_call | solution.py:438
Async XLA Ops:
  0.0 26.6 %copy-start.1 = (f32[1,1,3,32,512]{4,3,2,1,0:T(8,128)S(1)}, f32[1,1,3,32,512]{4,3,2,1,0:T(8,128)}, u32[]{:S(2)}) copy-start(f32[1,1,3,32,512]{4,3,2,1,0:T(8,128)} %param.8) | copy-start | bytes 589828
  1.8 24.8 %copy-start = (f32[1,1,4,32,512]{4,3,2,1,0:T(8,128)S(1)}, f32[1,1,4,32,512]{4,3,2,1,0:T(8,128)}, u32[]{:S(2)}) copy-start(f32[1,1,4,32,512]{4,3,2,1,0:T(8,128)} %param.7) | copy-start | bytes 786436
  1.8 24.7 %copy-start.2 = (s32[6,4,3]{0,1,2:T(4,128)S(1)}, s32[6,4,3]{0,1,2:T(4,128)}, u32[]{:S(2)}) copy-start(s32[6,4,3]{0,1,2:T(4,128)} %param.9) | copy-start | bytes 868
  1.8 25.0 %all-to-all-start = ((f32[12,24,128]{2,1,0:T(8,128)}), f32[12,24,128]{2,1,0:T(8,128)S(1)}, u32[]{:S(2)}, u32[]{:S(2)}) async-start(f32[12,24,128]{2,1,0:T(8,128)} %get-tuple-element.14), calls=%async_computation | async-start | bytes 294912 | tf_op jit(solution)/shard_map/all_to_all | solution.py:402
  18.6 12.0 %collective-permute-start = (f32[96,128]{1,0:T(8,128)S(1)}, f32[96,128]{1,0:T(8,128)S(1)}, u32[]{:S(2)}, u32[]{:S(2)}) collective-permute-start(f32[96,128]{1,0:T(8,128)S(1)} %get-tuple-element.12.after_ref.own_ref), channel_id=1, source_target_pairs={{0,16},{8,24},{16,0},{24,8},{32,48},{40,56},{48,32},{56,40},{64,80... | collective-permute-start | bytes 147464 | tf_op jit(solution)/shard_map/ppermute | solution.py:397
  39.6 5.7 %collective-permute-start.1 = (f32[4,192,128]{2,1,0:T(8,128)S(1)}, f32[4,192,128]{2,1,0:T(8,128)S(1)}, u32[]{:S(2)}, u32[]{:S(2)}) collective-permute-start(f32[4,192,128]{2,1,0:T(8,128)S(1)} %all_to_all.10.slot_ref), channel_id=1, source_target_pairs={{0,8},{8,0},{16,24},{24,16},{32,40},{40,32},{48,56},{56,48},{64,72... | collective-permute-start | bytes 1179656 | tf_op jit(solution)/shard_map/ppermute | solution.py:427

commit v8 on v7

--- a/solution.py
+++ b/solution.py
@@ -13,7 +13,7 @@
 META = 110
 FREE = 112
 LEAD = 11
-XLEAD = 2
+XORD = (2, 1, 3, 0)
 VMEM = pl.BlockSpec(memory_space=pltpu.VMEM)
 SMEM = pl.BlockSpec(memory_space=pltpu.SMEM)
 ANY = pl.BlockSpec(memory_space=pl.ANY)
@@ -26,6 +26,13 @@
 def place_of():
     t = lax.axis_index("tile")
     return t, t // 4, (t // 2) % 2, t % 2
+
+
+def order_of(x):
+    at = 0
+    for j in range(1, 4):
+        at = jnp.where(x == XORD[j], j, at)
+    return at
 
 
 def lane_rows(line):
@@ -230,7 +237,7 @@
     end_chip = 3 * z
     next_chip = jnp.where(z == 0, x + 1, x - 1)
     for j in range(4):
-        s = (XLEAD + j) % 4
+        s = XORD[j]
         side = side_ref[s]
         rows = jnp.where((next_chip == s) & (c != z), passed, 0.0)
         rows = jnp.where(end_chip == s, ends, rows)
@@ -316,7 +323,7 @@
 
 def near_kernel(slot_ref, inner_ref, end_ref, out_ref, halo_ref, total_ref):
     _, x, z, c = place_of()
-    halo = halo_sum(slot_ref, lax.rem(x + 4 - XLEAD, 4))
+    halo = halo_sum(slot_ref, order_of(x))
     halo_ref[0:8] = halo[0:8]
     halo_ref[8:24] = halo[8:24] + jnp.where((x == 3 * z) & (c == z), end_ref[...], 0.0)
     deposit(slot_ref, total_ref)
@@ -328,7 +335,7 @@
 def final_kernel(slot_ref, near_ref, halo_ref, courant_ref, out_ref, total_ref):
     _, x, z, c = place_of()
     halo = halo_ref[...] + halo_sum(slot_ref, -1)
-    chip = lax.rem(x + 4 - XLEAD, 4)
+    chip = order_of(x)
     kept = from_free([slot_ref[chip, WROWS * w : WROWS * w + 16, :] for w in range(8)])
     passed = jnp.concatenate([slot_ref[chip, WROWS * w + WIN : WROWS * (w + 1), :] for w in range(8)], 0)
     crossing = jnp.where(c == z, halo[8:24], passed)
@@ -422,7 +429,7 @@
         out_specs=VMEM,
         compiler_params=params,
     )(own, other, kept, side, ends, inner)
-    chips = [[tile_of((XLEAD + j) % 4, z, c) for j in range(4)] for z in range(2) for c in range(2)]
+    chips = [[tile_of(XORD[j], z, c) for j in range(4)] for z in range(2) for c in range(2)]
     near = lax.all_to_all(packed, "tile", 0, 0, tiled=True, axis_index_groups=chips)
     far = lax.ppermute(near, "tile", [(t, t ^ 1) for t in range(16)])
     scratch = [pltpu.VMEM((5, 88, 640), jnp.float32)]

time: 47 us -> 46.5 us (0.989)
  no operation moved by 1% of the time
where the time goes in v8:
time: 46.5 us; the launch traced here: 46.3 us
  starting transfers between devices  28.9 us (62%)
  blocking collectives  8.92 us (19%)
  Pallas kernels  4.88 us (10%)
  waiting for transfers between devices  3.46 us (7%)
    all_to_all x1, starting transfers between devices, body(): lax.all_to_all(slots, ('panel', 'tile'), 0, 0, tiled=True, axis_index_gro...  16.7 us
    all_to_all x1, blocking collectives, body(): lax.all_to_all(packed, 'tile', 0, 0, tiled=True, axis_index_groups=chips)  8.92 us
    ppermute x1, starting transfers between devices, body(): other = lax.ppermute(own, 'tile', [(t, t ^ 2) for t in range(16)])  7.93 us
    ppermute x1, starting transfers between devices, body(): far = lax.ppermute(near, 'tile', [(t, t ^ 1) for t in range(16)])  4.2 us
    ppermute x1, waiting for transfers between devices, body(): other = lax.ppermute(own, 'tile', [(t, t ^ 2) for t in range(16)])  2.62 us
    pallas_call x1, Pallas kernels, body(): pl.pallas_call(pool_kernel, out_shape=(shape(OWN, 128), shape(12, 24, 128...  1.81 us
    pallas_call x1, Pallas kernels, body(): pl.pallas_call(final_kernel, out_shape=shape(4, 32, 512), in_specs=[VMEM,...  1.21 us
    pallas_call x1, Pallas kernels, body(): pl.pallas_call(lines_kernel, out_shape=(shape(4, 8, 128), shape(16, 128))...  1.03 us
  transfers between devices with their start and end apart: 3, of which 2 were waited for; matrix products, arithmetic and copies ran while one was open for 0% of the time, Pallas kernels for 4%

profile of v8, /device:TPU:1, one launch (start us, length us, event | category | flops | bytes accessed | tf_op | source)
XLA Modules:
  0.0 46.3 jit_solution(2615587835945344520)
XLA Ops:
  0.0 0.0 copy-start.1
  0.0 1.8 %shard_map.73 = (f32[96,128]{1,0:T(8,128)S(1)}, f32[12,24,128]{2,1,0:T(8,128)}, f32[16,128]{1,0:T(8,128)S(1)}) custom-call(f32[4,128,128]{2,1,0:T(8,128)} %bitcast.18, f32[128,128]{1,0:T(8,128)} %bitcast.19, s32[4,4096]{1,0:T(4,128)} %bitcast.20, f32[4,32,512]{2,1,0:T(8,128)} %bitcast.14, s32[1,4]{1,0:T(1,128)} %live_hbm.1), custom_call_target="tpu_custom_call" | custom-call | tf_op jit(solution)/shard_map/pallas_call | solution.py:388
  1.8 0.0 copy-start
  1.8 0.0 copy-start.2
  1.8 16.7 %all-to-all-start = ((f32[12,24,128]{2,1,0:T(8,128)}), f32[12,24,128]{2,1,0:T(8,128)S(1)}, u32[]{:S(2)}, u32[]{:S(2)}) async-start(f32[12,24,128]{2,1,0:T(8,128)} %get-tuple-element.14), calls=%async_computation | async-start | bytes 294912 | tf_op jit(solution)/shard_map/all_to_all | solution.py:409
  18.6 7.9 %collective-permute-start = (f32[96,128]{1,0:T(8,128)S(1)}, f32[96,128]{1,0:T(8,128)S(1)}, u32[]{:S(2)}, u32[]{:S(2)}) collective-permute-start(f32[96,128]{1,0:T(8,128)S(1)} %get-tuple-element.12.after_ref.own_ref), channel_id=1, source_target_pairs={{0,16},{8,24},{16,0},{24,8},{32,48},{40,56},{48,32},{56,40},{64,80... | collective-permute-start | bytes 147464 | tf_op jit(solution)/shard_map/ppermute | solution.py:404
  26.5 0.0 copy-done.2
  26.5 0.1 copy.10.links_ref
  26.6 0.0 copy-done.1
  26.6 0.0 copy-done
  26.6 0.2 shard_map.75.after_ref.inner_ref
  26.9 0.0 all-to-all-done.slots_ref
  26.9 1.0 %shard_map.74 = (f32[4,8,128]{2,1,0:T(8,128)S(1)}, f32[16,128]{1,0:T(8,128)S(1)}) custom-call(f32[12,24,128]{2,1,0:T(8,128)S(1)} %all-to-all-done.slots_ref, s32[6,4,3]{2,1,0:T(4,128)S(1)} %copy.10.links_ref), custom_call_target="tpu_custom_call" | custom-call | tf_op jit(solution)/shard_map/pallas_call | solution.py:410
  27.9 2.6 %collective-permute-done.other_ref = f32[96,128]{1,0:T(8,128)S(1)} collective-permute-done((f32[96,128]{1,0:T(8,128)S(1)}, f32[96,128]{1,0:T(8,128)S(1)}, u32[]{:S(2)}, u32[]{:S(2)}) %collective-permute-start) | collective-permute-done | bytes 49184 | tf_op jit(solution)/shard_map/ppermute | solution.py:404
  30.5 0.1 shard_map.76
  30.7 8.9 %all_to_all.10.slot_ref = f32[4,192,128]{2,1,0:T(8,128)S(1)} all-to-all(f32[4,192,128]{2,1,0:T(8,128)S(1)} %shard_map.76), channel_id=1, replica_groups={{64,32,96,0},{72,40,104,8},{80,48,112,16},{88,56,120,24},{65,33,97,1},{..., dimensions={0} | all-to-all | bytes 786432 | tf_op jit(solution)/shard_map/all_to_all | solution.py:433
  39.6 4.2 %collective-permute-start.1 = (f32[4,192,128]{2,1,0:T(8,128)S(1)}, f32[4,192,128]{2,1,0:T(8,128)S(1)}, u32[]{:S(2)}, u32[]{:S(2)}) collective-permute-start(f32[4,192,128]{2,1,0:T(8,128)S(1)} %all_to_all.10.slot_ref), channel_id=1, source_target_pairs={{0,8},{8,0},{16,24},{24,16},{32,40},{40,32},{48,56},{56,48},{64,72... | collective-permute-start | bytes 1179656 | tf_op jit(solution)/shard_map/ppermute | solution.py:434
  43.8 0.5 %shard_map.77 = (f32[5,32,512]{2,1,0:T(8,128)S(1)}, f32[24,128]{1,0:T(8,128)S(1)}) custom-call(f32[4,192,128]{2,1,0:T(8,128)S(1)} %all_to_all.10.slot_ref, f32[4,32,512]{2,1,0:T(8,128)S(1)} %shard_map.75.after_ref.inner_ref, f32[16,128]{1,0:T(8,128)S(1)} %get-tuple-element.16.ends_ref.end_ref), custom_call_target="tpu_custom_call" | custom-call | flops 1048576 | bytes 1048576 | tf_op jit(solution)/shard_map/pallas_call | solution.py:436
  44.3 0.8 %collective-permute-done.1.slot_ref = f32[4,192,128]{2,1,0:T(8,128)S(1)} collective-permute-done((f32[4,192,128]{2,1,0:T(8,128)S(1)}, f32[4,192,128]{2,1,0:T(8,128)S(1)}, u32[]{:S(2)}, u32[]{:S(2)}) %collective-permute-start.1) | collective-permute-done | bytes 393248 | tf_op jit(solution)/shard_map/ppermute | solution.py:434
  45.1 1.2 %shard_map.78 = f32[4,32,512]{2,1,0:T(8,128)} custom-call(f32[4,192,128]{2,1,0:T(8,128)S(1)} %collective-permute-done.1.slot_ref, f32[5,32,512]{2,1,0:T(8,128)S(1)} %get-tuple-element.17.near_ref, f32[24,128]{1,0:T(8,128)S(1)} %get-tuple-element.18.halo_ref, f32[3,32,512]{2,1,0:T(8,128)S(1)} %bitcast.17), custom_call_target="tpu_custom_call" | custom-call | tf_op jit(solution)/shard_map/pallas_call | solution.py:445
Async XLA Ops:
  0.0 26.6 %copy-start.1 = (f32[1,1,3,32,512]{4,3,2,1,0:T(8,128)S(1)}, f32[1,1,3,32,512]{4,3,2,1,0:T(8,128)}, u32[]{:S(2)}) copy-start(f32[1,1,3,32,512]{4,3,2,1,0:T(8,128)} %param.8) | copy-start | bytes 589828
  1.8 24.8 %copy-start = (f32[1,1,4,32,512]{4,3,2,1,0:T(8,128)S(1)}, f32[1,1,4,32,512]{4,3,2,1,0:T(8,128)}, u32[]{:S(2)}) copy-start(f32[1,1,4,32,512]{4,3,2,1,0:T(8,128)} %param.7) | copy-start | bytes 786436
  1.8 24.7 %copy-start.2 = (s32[6,4,3]{0,1,2:T(4,128)S(1)}, s32[6,4,3]{0,1,2:T(4,128)}, u32[]{:S(2)}) copy-start(s32[6,4,3]{0,1,2:T(4,128)} %param.9) | copy-start | bytes 868
  1.8 25.0 %all-to-all-start = ((f32[12,24,128]{2,1,0:T(8,128)}), f32[12,24,128]{2,1,0:T(8,128)S(1)}, u32[]{:S(2)}, u32[]{:S(2)}) async-start(f32[12,24,128]{2,1,0:T(8,128)} %get-tuple-element.14), calls=%async_computation | async-start | bytes 294912 | tf_op jit(solution)/shard_map/all_to_all | solution.py:409
  18.6 12.0 %collective-permute-start = (f32[96,128]{1,0:T(8,128)S(1)}, f32[96,128]{1,0:T(8,128)S(1)}, u32[]{:S(2)}, u32[]{:S(2)}) collective-permute-start(f32[96,128]{1,0:T(8,128)S(1)} %get-tuple-element.12.after_ref.own_ref), channel_id=1, source_target_pairs={{0,16},{8,24},{16,0},{24,8},{32,48},{40,56},{48,32},{56,40},{64,80... | collective-permute-start | bytes 147464 | tf_op jit(solution)/shard_map/ppermute | solution.py:404
  39.6 5.5 %collective-permute-start.1 = (f32[4,192,128]{2,1,0:T(8,128)S(1)}, f32[4,192,128]{2,1,0:T(8,128)S(1)}, u32[]{:S(2)}, u32[]{:S(2)}) collective-permute-start(f32[4,192,128]{2,1,0:T(8,128)S(1)} %all_to_all.10.slot_ref), channel_id=1, source_target_pairs={{0,8},{8,0},{16,24},{24,16},{32,40},{40,32},{48,56},{56,48},{64,72... | collective-permute-start | bytes 1179656 | tf_op jit(solution)/shard_map/ppermute | solution.py:434
